TPU v7x, 32 devices: a whole 2x2x4 slice. The times are simulated.
32 devices in a mesh: dp: 8 (over z, y), ctx: 4 (over x, core).
Axes of the slice: x: 2, y: 2, z: 4, core: 2. Of those that a mesh axis runs over, the one named last changes fastest.
Arguments:
- block_input: bfloat16 [8, 2048, 896], P('dp', 'ctx'), may hold values from -6 to 6
- cotangent: bfloat16 [8, 2048, 896], P('dp', 'ctx'), may hold values from -6 to 6
- lengths: int32 [8], P('dp'), may hold values from 1537 to 2048, as said below
- doc_starts: int32 [8], P('dp'), may hold values from 128 to 511
- master: float32 [32, 465920], P(('dp', 'ctx'))
- momentum: float32 [32, 465920], P(('dp', 'ctx'))
- vectors: float32 [32, 92], P(('dp', 'ctx'))
- vector_first: float32 [32, 92], P(('dp', 'ctx'))
- vector_second: float32 [32, 92], P(('dp', 'ctx'))
Outputs:
- layer_out: bfloat16 [8, 2048, 896], P('dp', 'ctx')
- input_grad: bfloat16 [8, 2048, 896], P('dp', 'ctx')
- new_master: float32 [32, 465920], P(('dp', 'ctx'))
- new_momentum: float32 [32, 465920], P(('dp', 'ctx'))
- master_copy: bfloat16 [32, 465920], P(('dp', 'ctx'))
- new_vectors: float32 [32, 92], P(('dp', 'ctx'))
- first_moment: float32 [32, 92], P(('dp', 'ctx'))
- second_moment: float32 [32, 92], P(('dp', 'ctx'))
Inputs may be any that keep to these rules, and one draw needn't show every extreme that they name: `lengths`: in every draw some slot is used to its end.
All inputs are finite; a program needn't handle non-finite values.
Results may differ from a plain program's by a relative error of at most 0.014.
Values may be sent and summed in bfloat16 or wider, within the bound.
No kernel may reach another device: no remote copies, remote signals or barrier semaphores. Data moves between devices by JAX's collectives and lax.ppermute only.
A program may use at most 384 MiB of HBM per device.

v0:
```python
import math

import jax
import jax.numpy as jnp
from jax import lax
from jax.experimental import pallas as pl
from jax.experimental.pallas import tpu as pltpu
from jax.sharding import PartitionSpec as P

D = 896
HEADS = 14
KVH = 2
HD = 64
FF = 4864
SLOT = 2048
NS_STEPS = 3
STEP = 10
QD = 896
KVD = 128

NORM_EPS = 1e-06
ROPE_BASE = 1000000.0
NS_LINEAR = 3.4445
NS_SQUARE = -4.775
NS_CUBIC = 2.0315
MOMENTUM_DECAY = 0.5
MUON_RATE = 0.6
MUON_DECAY = 0.1
ADAM_RATE = 0.2
BETA_FIRST = 0.9
BETA_SECOND = 0.95
ADAM_EPS = 1e-08
MASK_FLOOR = -1e30

F32 = jnp.float32
BF16 = jnp.bfloat16
BOTH = ("dp", "ctx")
LANES = 128


def matrix_shapes():
    return [(D, QD), (D, KVD), (D, KVD), (QD, D), (D, FF), (D, FF), (FF, D)]


def vector_sizes():
    return [D, D, QD, KVD, KVD]


def mm(left, right, contract=((1,), (0,))):
    return lax.dot_general(left, right, (contract, ((), ())), preferred_element_type=F32)


def split_small(flat, devices):
    result = []
    offset = 0
    for extent_all in vector_sizes():
        extent = extent_all // devices
        result.append(flat[:, offset : offset + extent].reshape(extent_all))
        offset += extent
    return result


def join_small(pieces, devices):
    return jnp.concatenate([piece.reshape(devices, -1) for piece in pieces], axis=1)


def swap(value, mask, devices):
    return lax.ppermute(value, BOTH, [(index, index ^ mask) for index in range(devices)])


def gather_bits(value, bits, me, devices, before=()):
    held = value
    done = list(before)
    for bit in bits:
        place = sum(1 for other in done if other > bit)
        got = swap(held, bit, devices)
        mine = (me & bit) != 0
        held = jnp.where(
            mine, jnp.stack([got, held], axis=place), jnp.stack([held, got], axis=place)
        )
        done.append(bit)
    return held


def scatter_split(held, left, bit, me, lead=0):
    axis = sorted(left, reverse=True).index(bit) + lead
    mine = jnp.where((me & bit) != 0, 1, 0)
    return choose(held, 1 - mine, axis).astype(BF16), choose(held, mine, axis)


def scatter_start(held, left, bit, me, devices):
    sent, kept = scatter_split(held, left, bit, me)
    return kept, swap(sent, bit, devices)


def scatter_end(parts):
    return (parts[0].astype(F32) + parts[1].astype(F32)).astype(BF16)


def scatter_sum(value, bits, me, devices):
    left = list(bits)
    held = value
    for bit in bits:
        held = scatter_end(scatter_start(held, left, bit, me, devices))
        left.remove(bit)
    return held


def choose(value, mine, axis):
    return lax.dynamic_index_in_dim(value, mine, axis, keepdims=False)


def rotate(values, cosine, sine_part):
    midpoint = HD // 2
    turned = jnp.concatenate([-values[:, midpoint:], values[:, :midpoint]], axis=1)
    return values * cosine + turned * sine_part


def rotate_back(gradient, cosine, sine_part):
    midpoint = HD // 2
    scaled = gradient * sine_part
    turned = jnp.concatenate([scaled[:, midpoint:], -scaled[:, :midpoint]], axis=1)
    return gradient * cosine + turned


def norm_backward(source, scale_row, gain, incoming):
    gain_grad = jnp.sum(incoming * source * scale_row, axis=0)
    weighted = incoming * gain
    result = scale_row * weighted - source * scale_row**3 * jnp.mean(
        weighted * source, axis=-1, keepdims=True
    )
    return (result, gain_grad)


def halves_of(span):
    return [slice(0, span // 2), slice(span // 2, span)]


def fill_mask(info, mask, chunk, span):
    key = chunk * span + lax.broadcasted_iota(jnp.int32, (span, span), 0)
    query = info[0] * span + lax.broadcasted_iota(jnp.int32, (span, span), 1)
    key_doc = (key >= info[2]).astype(jnp.int32) + (key >= info[1]).astype(jnp.int32)
    query_doc = (query >= info[2]).astype(jnp.int32) + (query >= info[1]).astype(jnp.int32)
    allowed = jnp.logical_and(key_doc == query_doc, key <= query)
    mask[chunk] = jnp.where(allowed, 0.0, MASK_FLOOR).astype(F32)


def attend_kernel(info, kv, q, out, lse, keys, mask, best, total, acc):
    head = pl.program_id(0)
    span = q.shape[-1]
    mine = info[0]
    chunks = mine + 1

    @pl.when(head == 0)
    def _():
        def fill(chunk, carry):
            slot = jnp.bitwise_xor(chunk, mine)
            keys[chunk] = kv[slot, :HD, :].astype(F32).T.astype(BF16)
            fill_mask(info, mask, chunk, span)
            return carry

        lax.fori_loop(0, chunks, fill, 0)

    best[...] = jnp.full(best.shape, MASK_FLOOR, F32)
    total[...] = jnp.zeros(total.shape, F32)
    acc[...] = jnp.zeros(acc.shape, F32)
    queries = q[0]

    def step(index, carry):
        chunk = mine - index
        slot = jnp.bitwise_xor(chunk, mine)
        scores = jnp.dot(keys[chunk], queries, preferred_element_type=F32) + mask[chunk]
        old = best[...]
        new = jnp.maximum(old, jnp.max(scores, axis=0, keepdims=True))
        present = jnp.exp(scores - new)
        shrink = jnp.exp(old - new)
        best[...] = new
        total[...] = total[...] * shrink + jnp.sum(present, axis=0, keepdims=True)
        acc[...] = acc[...] * shrink + jnp.dot(
            kv[slot, HD:, :], present.astype(BF16), preferred_element_type=F32
        )
        return carry

    lax.fori_loop(0, chunks, step, 0)
    out[0] = acc[...] / total[...]
    lse[0] = best[...] + jnp.log(total[...])


def attend_back_kernel(
    info, kv, q, dout, lse, delta, before, dq, dkv, keys, values, mask, dk, dv, acc
):
    head = pl.program_id(0)
    span = q.shape[-1]
    mine = info[0]
    chunks = mine + 1
    n_ctx = kv.shape[0]

    @pl.when(head == 0)
    def _():
        dk[...] = jnp.zeros(dk.shape, F32)
        dv[...] = jnp.zeros(dv.shape, F32)

        def fill(chunk, carry):
            slot = jnp.bitwise_xor(chunk, mine)
            keys[chunk] = kv[slot, :HD, :].astype(F32).T.astype(BF16)
            values[chunk] = kv[slot, HD:, :].astype(F32).T.astype(BF16)
            fill_mask(info, mask, chunk, span)
            return carry

        lax.fori_loop(0, chunks, fill, 0)

    acc[...] = jnp.zeros(acc.shape, F32)
    queries = q[0]
    douts = dout[0]
    query_rows = queries.astype(F32).T.astype(BF16)
    dout_rows = douts.astype(F32).T.astype(BF16)

    def step(chunk, carry):
        slot = jnp.bitwise_xor(chunk, mine)
        value_sum, key_sum = dv[chunk], dk[chunk]
        for lanes in halves_of(span):
            scores = (
                jnp.dot(keys[chunk], queries[:, lanes], preferred_element_type=F32)
                + mask[chunk, :, lanes]
            )
            shares = jnp.exp(scores - lse[0, :, lanes])
            share_grad = jnp.dot(values[chunk], douts[:, lanes], preferred_element_type=F32)
            score_grad = (shares * (share_grad - delta[0, :, lanes])).astype(BF16)
            value_sum += jnp.dot(
                shares.astype(BF16), dout_rows[lanes, :], preferred_element_type=F32
            )
            key_sum += jnp.dot(score_grad, query_rows[lanes, :], preferred_element_type=F32)
            acc[:, lanes] += jnp.dot(kv[slot, :HD, :], score_grad, preferred_element_type=F32)
        dv[chunk], dk[chunk] = value_sum, key_sum
        return carry

    lax.fori_loop(0, chunks, step, 0)
    dq[0] = acc[...] * HD ** (-0.5)

    @pl.when(head == pl.num_programs(0) - 1)
    def _():
        for chunk in range(n_ctx):
            sums = jnp.concatenate([dk[chunk].T, dv[chunk].T], axis=0)
            if before is not None:
                sums += before[chunk].astype(F32)
            dkv[chunk] = sums.astype(BF16)


def attend(info, kv, q):
    heads, _, span = q.shape
    n_ctx = kv.shape[0]
    per_head = lambda rows: pl.BlockSpec((1, rows, span), lambda head: (head, 0, 0))
    return pl.pallas_call(
        attend_kernel,
        grid=(heads,),
        in_specs=[
            pl.BlockSpec(memory_space=pltpu.SMEM),
            pl.BlockSpec(kv.shape, lambda head: (0, 0, 0)),
            per_head(HD),
        ],
        out_specs=[per_head(HD), per_head(1)],
        out_shape=[
            jax.ShapeDtypeStruct((heads, HD, span), F32),
            jax.ShapeDtypeStruct((heads, 1, span), F32),
        ],
        scratch_shapes=[
            pltpu.VMEM((n_ctx, span, HD), BF16),
            pltpu.VMEM((n_ctx, span, span), F32),
            pltpu.VMEM((1, span), F32),
            pltpu.VMEM((1, span), F32),
            pltpu.VMEM((HD, span), F32),
        ],
        compiler_params=pltpu.CompilerParams(vmem_limit_bytes=40 * 1024 * 1024),
        cost_estimate=pl.CostEstimate(
            flops=4 * heads * span * span * n_ctx * HD * 4,
            bytes_accessed=4 * heads * span * HD * 2,
            transcendentals=heads * span * span * n_ctx,
        ),
        name="attend",
    )(info, kv, q)


def attend_back(info, kv, q, dout, lse, delta, before):
    heads, _, span = q.shape
    n_ctx = kv.shape[0]
    per_head = lambda rows: pl.BlockSpec((1, rows, span), lambda head: (head, 0, 0))
    whole = pl.BlockSpec(kv.shape, lambda head: (0, 0, 0))
    if before is None:
        body = lambda *refs: attend_back_kernel(*refs[:6], None, *refs[6:])
    else:
        body = attend_back_kernel
    return pl.pallas_call(
        body,
        grid=(heads,),
        in_specs=[
            pl.BlockSpec(memory_space=pltpu.SMEM),
            whole,
            per_head(HD),
            per_head(HD),
            per_head(1),
            per_head(1),
        ]
        + [whole] * (before is not None),
        out_specs=[per_head(HD), whole],
        out_shape=[
            jax.ShapeDtypeStruct((heads, HD, span), F32),
            jax.ShapeDtypeStruct(kv.shape, BF16),
        ],
        scratch_shapes=[
            pltpu.VMEM((n_ctx, span, HD), BF16),
            pltpu.VMEM((n_ctx, span, HD), BF16),
            pltpu.VMEM((n_ctx, span, span), F32),
            pltpu.VMEM((n_ctx, span, HD), F32),
            pltpu.VMEM((n_ctx, span, HD), F32),
            pltpu.VMEM((HD, span), F32),
        ],
        compiler_params=pltpu.CompilerParams(vmem_limit_bytes=40 * 1024 * 1024),
        cost_estimate=pl.CostEstimate(
            flops=10 * heads * span * span * n_ctx * HD * 4,
            bytes_accessed=8 * heads * span * HD * 2,
            transcendentals=heads * span * span * n_ctx,
        ),
        name="attend_back",
    )(*[info, kv, q, dout, lse, delta] + [before] * (before is not None))


def forward_backward_kernel(
    x0, x1, dy0, dy1, wide, down, act_out, both_out, x_out, dy_out, back0, back1
):
    first = pl.program_id(0) == 0
    units = down.shape[0]
    x = jnp.where(first, x0[...], x1[...])
    dy = jnp.where(first, dy0[...], dy1[...])
    x_out[...] = x
    dy_out[...] = dy
    both = jnp.dot(x, wide[...], preferred_element_type=F32)
    gate_pre = both[:, :units]
    up_pre = both[:, units:]
    grad_act = mm(dy, down[...], ((1,), (1,)))
    sigmoid_gate = jax.nn.sigmoid(gate_pre)
    swish = gate_pre * sigmoid_gate
    slope = sigmoid_gate * (1.0 + gate_pre * (1.0 - sigmoid_gate))
    act_out[...] = (swish * up_pre).astype(BF16)
    both_back = jnp.concatenate([grad_act * up_pre * slope, grad_act * swish], axis=1).astype(BF16)
    both_out[...] = both_back
    back = mm(both_back, wide[...], ((1,), (1,))).astype(BF16)

    @pl.when(first)
    def _():
        back0[...] = back

    @pl.when(jnp.logical_not(first))
    def _():
        back1[...] = back


def feed_forward(x, dy, wide, down, blocks, earlier):
    span, width = x[0].shape
    units = down.shape[0]
    first = 0 if earlier is None else 2
    whole = lambda shape: pl.BlockSpec(
        shape, lambda block: (0, 0), pipeline_mode=pl.Buffered(1)
    )
    line = lambda columns: pl.BlockSpec((span, columns), lambda block: (block + first, 0))
    columns = [units, 2 * units, width, width]
    shapes = [jax.ShapeDtypeStruct((blocks * span, count), BF16) for count in columns]
    in_specs = [whole((span, width))] * 4 + [whole((width, 2 * units)), whole((units, width))]
    operands = [*x, *dy, wide, down]
    aliases = {}
    body = forward_backward_kernel
    if earlier is not None:
        in_specs += [pl.BlockSpec(memory_space=pl.ANY)] * 4
        operands += list(earlier)
        aliases = {6 + index: index for index in range(4)}
        body = lambda *refs: forward_backward_kernel(*refs[:6], *refs[10:])
    back = pl.BlockSpec((span, width), lambda block: (0, 0))
    results = pl.pallas_call(
        body,
        grid=(2,),
        in_specs=in_specs,
        out_specs=[line(count) for count in columns] + [back, back],
        out_shape=shapes + [jax.ShapeDtypeStruct((span, width), BF16)] * 2,
        input_output_aliases=aliases,
        compiler_params=pltpu.CompilerParams(vmem_limit_bytes=60 * 1024 * 1024),
        cost_estimate=pl.CostEstimate(
            flops=20 * span * width * units,
            bytes_accessed=6 * width * units + 2 * span * 10 * width,
            transcendentals=2 * span * units,
        ),
        name="feed_forward",
    )(*operands)
    return results[:4], results[4:]


BLOCK = 128


def block_pairs(count):
    return [(low, high) for low in range(count) for high in range(low, count)]


def gram_kernel(rows, out):
    count = rows.shape[1] // BLOCK
    place = 0
    for low in range(count):
        line = lax.dot_general(
            rows[:, low * BLOCK : (low + 1) * BLOCK],
            rows[:, low * BLOCK :],
            (((0,), (0,)), ((), ())),
            preferred_element_type=F32,
        ).astype(BF16)
        for high in range(low, count):
            out[place] = line[:, (high - low) * BLOCK : (high - low + 1) * BLOCK]
            place += 1
    for extra in range(place, out.shape[0]):
        out[extra] = jnp.zeros((BLOCK, BLOCK), BF16)


def gram_blocks(rows, places):
    return pl.pallas_call(
        gram_kernel,
        out_shape=jax.ShapeDtypeStruct((places, BLOCK, BLOCK), BF16),
        compiler_params=pltpu.CompilerParams(vmem_limit_bytes=32 * 1024 * 1024),
        name="gram",
    )(rows)


def newton_schulz(gram, low, poly, mixed, rows):
    size = gram.shape[0]
    part = size // 2 if size % 16 == 0 and size > BLOCK else size
    parts = [pl.ds(begin, part) for begin in range(0, size, part)]
    row_id = lax.broadcasted_iota(jnp.int32, (size, size), 0)
    column_id = lax.broadcasted_iota(jnp.int32, (size, size), 1)
    square = jnp.where(row_id == column_id, gram[...], 0.0)
    square = jnp.sum(jnp.sum(square, axis=0, keepdims=True), axis=1, keepdims=True)
    scale = 1.0 / (jnp.sqrt(square) + 1e-07)
    for place in parts:
        scaled = gram[place, :] * (scale * scale)
        gram[place, :] = scaled
        low[place, :] = scaled.astype(BF16)
    work = (rows * scale).astype(BF16)
    for step in range(NS_STEPS):
        for place in parts:
            second = jnp.dot(low[place, :], low[...], preferred_element_type=F32)
            poly[place, :] = (NS_SQUARE * gram[place, :] + NS_CUBIC * second).astype(BF16)
        moved = jnp.dot(work, poly[...], preferred_element_type=F32)
        work = (NS_LINEAR * work.astype(F32) + moved).astype(BF16)
        if step + 1 < NS_STEPS:
            for place in parts:
                first = jnp.dot(poly[place, :], low[...], preferred_element_type=F32)
                mixed[place, :] = first.astype(BF16)
                gram[place, :] = (
                    NS_LINEAR * NS_LINEAR * gram[place, :] + (2.0 * NS_LINEAR) * first
                )
            for place in parts:
                second = jnp.dot(poly[place, :], mixed[...], preferred_element_type=F32)
                renewed = gram[place, :] + second
                gram[place, :] = renewed
                low[place, :] = renewed.astype(BF16)
    return work


def wide_kernel(blocks, rows, out, gram, low, poly, mixed):
    for place, (first, second) in enumerate(block_pairs(gram.shape[0] // BLOCK)):
        tile = blocks[place].astype(F32)
        gram[first * BLOCK : (first + 1) * BLOCK, second * BLOCK : (second + 1) * BLOCK] = tile
        if first != second:
            gram[second * BLOCK : (second + 1) * BLOCK, first * BLOCK : (first + 1) * BLOCK] = tile.T
    out[...] = newton_schulz(gram, low, poly, mixed, rows[...].astype(F32))


def square_scratch(size):
    return [
        pltpu.VMEM((size, size), F32),
        pltpu.VMEM((size, size), BF16),
        pltpu.VMEM((size, size), BF16),
        pltpu.VMEM((size, size), BF16),
    ]


def orthogonal_wide(blocks, rows):
    return pl.pallas_call(
        wide_kernel,
        out_shape=jax.ShapeDtypeStruct(rows.shape, BF16),
        scratch_shapes=square_scratch(rows.shape[1]),
        compiler_params=pltpu.CompilerParams(vmem_limit_bytes=40 * 1024 * 1024),
        cost_estimate=pl.CostEstimate(
            flops=14 * rows.shape[1] ** 3, bytes_accessed=4 * rows.size, transcendentals=0
        ),
        name="newton_wide",
    )(blocks, rows)


def whole_kernel(widths, whole, rows, out, *scratch):
    begin = 0
    for index, width in enumerate(widths):
        gram, low, poly, mixed = scratch[4 * index : 4 * index + 4]
        for first in range(0, width, BLOCK):
            gram[first : first + BLOCK, :] = lax.dot_general(
                whole[:, begin + first : begin + first + BLOCK],
                whole[:, begin : begin + width],
                (((0,), (0,)), ((), ())),
                preferred_element_type=F32,
            )
        out[:, begin : begin + width] = newton_schulz(
            gram, low, poly, mixed, rows[:, begin : begin + width]
        )
        begin += width


def orthogonal_whole(whole, rows, widths):
    scratch = []
    for width in widths:
        scratch += square_scratch(width)
    return pl.pallas_call(
        lambda *refs: whole_kernel(widths, *refs),
        out_shape=jax.ShapeDtypeStruct(rows.shape, BF16),
        scratch_shapes=scratch,
        compiler_params=pltpu.CompilerParams(vmem_limit_bytes=48 * 1024 * 1024),
        cost_estimate=pl.CostEstimate(
            flops=16 * sum(width**3 for width in widths),
            bytes_accessed=2 * whole.size,
            transcendentals=0,
        ),
        name="newton_whole",
    )(whole, rows)


def from_flat(flat, base, target, height, breadth):
    lines = breadth // LANES
    for begin in range(0, height, 8):
        count = min(8, height - begin)
        for index in range(lines):
            start = base + begin * lines + index
            if lines == 1:
                tile = flat[start : start + count, :]
            else:
                tile = flat[pl.ds(start, count, stride=lines), :]
            target[begin : begin + count, index * LANES : (index + 1) * LANES] = tile


def to_flat(flat, base, value, height, breadth):
    lines = breadth // LANES
    for begin in range(0, height, 8):
        count = min(8, height - begin)
        for index in range(lines):
            start = base + begin * lines + index
            tile = value(slice(begin, begin + count), slice(index * LANES, (index + 1) * LANES))
            if lines == 1:
                flat[start : start + count, :] = tile
            else:
                flat[pl.ds(start, count, stride=lines), :] = tile


def section_bases(devices):
    bases = []
    base = 0
    for height, breadth in matrix_shapes():
        bases.append(base)
        base += height // devices * breadth // LANES
    return bases


def pack_kernel(devices, group, flat, extra, qkv_out, out_out, wide_out, down_out, qkv, out, wide, down):
    rows = D // devices
    frows = FF // devices
    bases = section_bases(devices)
    qkv[...] = jnp.zeros(qkv.shape, F32)
    out[...] = jnp.zeros(out.shape, F32)
    from_flat(flat, bases[0], qkv.at[:, :QD], rows, QD)
    from_flat(flat, bases[1], qkv.at[:, QD : QD + KVD], rows, KVD)
    from_flat(flat, bases[2], qkv.at[:, QD + KVD :], rows, KVD)
    if extra is not None:
        qkv[rows : rows + 1, :LANES] = extra[...]
    from_flat(flat, bases[3], out, rows, D)
    from_flat(flat, bases[6], down, FF // devices, D)
    qkv_out[...] = qkv[...].astype(qkv_out.dtype)
    out_out[...] = out[...].astype(out_out.dtype)
    down_out[...] = down[...].astype(down_out.dtype)
    for which in range(2):
        from_flat(flat, bases[4 + which], wide, rows, FF)
        targets = devices // group
        for target in range(targets):
            piece = jnp.concatenate(
                [
                    wide[:, (turn * targets + target) * frows : (turn * targets + target + 1) * frows]
                    for turn in range(group)
                ],
                axis=1,
            )
            width = group * frows
            wide_out[target, :, which * width : (which + 1) * width] = piece.astype(wide_out.dtype)


def pack(flat, extra, devices, group, dtype):
    rows = D // devices
    frows = FF // devices
    padded = (rows // 16 + 1) * 16
    targets = devices // group
    wide = (targets, rows, 2 * group * frows)
    shapes = [(padded, QD + 2 * KVD), (padded, D), wide, (frows, D)]
    types = [dtype, dtype, BF16, dtype]
    if extra is None:
        body = lambda flat_ref, *refs: pack_kernel(devices, group, flat_ref, None, *refs)
        operands = [flat]
    else:
        body = lambda *refs: pack_kernel(devices, group, *refs)
        operands = [flat, extra]
    return pl.pallas_call(
        body,
        out_shape=[jax.ShapeDtypeStruct(shape, kind) for shape, kind in zip(shapes, types)],
        scratch_shapes=[
            pltpu.VMEM((padded, QD + 2 * KVD), F32),
            pltpu.VMEM((padded, D), F32),
            pltpu.VMEM((rows, FF), F32),
            pltpu.VMEM((frows, D), F32),
        ],
        compiler_params=pltpu.CompilerParams(vmem_limit_bytes=32 * 1024 * 1024),
        cost_estimate=pl.CostEstimate(flops=0, bytes_accessed=6 * flat.size, transcendentals=0),
        name="pack",
    )(*operands)


def update_kernel(devices, decay, factors, flat, qkv, out, wide, down, result, moved, rows_wide):
    rows = D // devices
    frows = FF // devices
    bases = section_bases(devices)
    whole = qkv[...].astype(F32)
    out_whole = out[...].astype(F32)
    down_whole = down[...].astype(F32)
    parts = [
        lambda r, c: whole[r, c],
        lambda r, c: whole[r, slice(QD + c.start, QD + c.stop)],
        lambda r, c: whole[r, slice(QD + KVD + c.start, QD + KVD + c.stop)],
        lambda r, c: out_whole[r, c],
    ]
    shapes = matrix_shapes()
    for index, part in enumerate(parts):
        to_flat(
            moved, bases[index], lambda r, c: part(r, c) * factors[index], rows, shapes[index][1]
        )
    to_flat(moved, bases[6], lambda r, c: down_whole[r, c] * factors[6], frows, D)
    for which in range(2):
        for source in range(devices):
            rows_wide[:, source * frows : (source + 1) * frows] = wide[
                source, :, which * frows : (which + 1) * frows
            ].astype(F32)
        to_flat(
            moved, bases[4 + which], lambda r, c: rows_wide[r, c] * factors[4 + which], rows, FF
        )
    result[...] = decay * flat[...] + moved[...]


def update(flat, qkv, out, wide, down, devices, decay, factors):
    return pl.pallas_call(
        lambda *refs: update_kernel(devices, decay, factors, *refs),
        out_shape=jax.ShapeDtypeStruct(flat.shape, F32),
        scratch_shapes=[
            pltpu.VMEM(flat.shape, F32),
            pltpu.VMEM((D // devices, FF), F32),
        ],
        compiler_params=pltpu.CompilerParams(vmem_limit_bytes=32 * 1024 * 1024),
        cost_estimate=pl.CostEstimate(flops=0, bytes_accessed=10 * flat.size, transcendentals=0),
        name="update",
    )(flat, qkv, out, wide, down)


def combine_kernel(old_pair, gate, up, old_down, down, old_out, out, mats, lines):
    devices, rows, _ = old_pair.shape
    frows = gate.shape[0]
    padded = out.shape[0]
    lines[...] = jnp.zeros(lines.shape, F32)
    for source in range(devices):
        lines[source * rows : (source + 1) * rows, : 2 * frows] = old_pair[source].astype(F32)
    old = lines[...].T
    mats[0] = (MOMENTUM_DECAY * old[:frows] + gate[...].astype(F32)).astype(BF16)
    mats[1] = (MOMENTUM_DECAY * old[frows : 2 * frows] + up[...].astype(F32)).astype(BF16)
    mats[2] = (MOMENTUM_DECAY * old_down[...] + down[...].astype(F32)).astype(BF16)
    last = MOMENTUM_DECAY * old_out[...] + out[...].astype(F32)
    mats[3] = jnp.concatenate(
        [last, jnp.zeros((frows - padded, last.shape[1]), F32)], axis=0
    ).astype(BF16)


def combine(old_pair, gate, up, old_down, down, old_out, out):
    frows, width = gate.shape
    return pl.pallas_call(
        combine_kernel,
        out_shape=jax.ShapeDtypeStruct((4, frows, width), BF16),
        scratch_shapes=[pltpu.VMEM((width, -(-2 * frows // LANES) * LANES), F32)],
        compiler_params=pltpu.CompilerParams(vmem_limit_bytes=32 * 1024 * 1024),
        name="combine",
    )(old_pair, gate, up, old_down, down, old_out, out)


def turn_kernel(gate, up, out, columns):
    devices, rows, _ = out.shape
    frows = gate.shape[0]
    columns[...] = jnp.zeros(columns.shape, F32)
    columns[:frows] = gate[...].astype(F32)
    columns[frows : 2 * frows] = up[...].astype(F32)
    lines = columns[...].T
    for target in range(devices):
        out[target] = lines[target * rows : (target + 1) * rows, : 2 * frows].astype(BF16)


def turn(gate, up, devices):
    frows, width = gate.shape
    return pl.pallas_call(
        turn_kernel,
        out_shape=jax.ShapeDtypeStruct((devices, width // devices, 2 * frows), BF16),
        scratch_shapes=[pltpu.VMEM((-(-2 * frows // LANES) * LANES, width), F32)],
        compiler_params=pltpu.CompilerParams(vmem_limit_bytes=32 * 1024 * 1024),
        name="turn",
    )(gate, up)


def on_device(
    block_input,
    cotangent,
    lengths,
    doc_starts,
    master,
    momentum,
    vectors,
    vector_first,
    vector_second,
):
    n_dp = lax.axis_size("dp")
    n_ctx = lax.axis_size("ctx")
    devices = n_dp * n_ctx
    rows = D // devices
    frows = FF // devices
    fblock = FF // n_ctx
    slots, span, width = block_input.shape
    tokens = slots * span
    group = HEADS // KVH
    qkv = QD + 2 * KVD
    my_ctx = lax.axis_index("ctx")
    me = lax.axis_index("dp") * n_ctx + my_ctx
    core_bit, x_bit = 1, 2
    ctx_bits = [core_bit, x_bit]
    dp_bits = [n_ctx << index for index in range(n_dp.bit_length() - 1)]
    all_bits = ctx_bits + dp_bits
    many = tuple([2] * len(all_bits))
    padded = (rows // 16 + 1) * 16

    master_flat = master.reshape(-1, LANES)
    momentum_flat = momentum.reshape(-1, LANES)
    small = jnp.pad(vectors, ((0, 0), (0, LANES - vectors.shape[1])))
    qkv_local, out_local, gate_up, down_local = pack(master_flat, small, devices, n_dp, BF16)

    attn_full = gather_bits(
        jnp.concatenate([qkv_local, out_local], axis=1), dp_bits[::-1], me, devices
    )
    down_bits = dp_bits[::-1]
    down_part, attn_full = lax.optimization_barrier((down_local, attn_full))
    high, low = down_bits[:2]
    down_came = [swap(down_part, mask, devices) for mask in (low, high, high + low)]
    qkv_full = gather_bits(attn_full[..., :qkv], ctx_bits[::-1], me, devices, dp_bits)
    qkv_full = qkv_full.reshape(devices, padded, qkv)
    gain_first, gain_second, bias_query, bias_key, bias_value = [
        piece.astype(F32) for piece in split_small(qkv_full[:, rows], devices)
    ]
    w_qkv = qkv_full[:, :rows].reshape(D, qkv)

    came = [choose(gate_up, my_ctx, 0)] + [
        swap(choose(gate_up, my_ctx ^ mask, 0), mask, devices) for mask in range(1, n_ctx)
    ]
    came, attn_full = lax.optimization_barrier((came, attn_full))
    ordered = []
    for source in range(n_ctx):
        piece = came[0]
        for mask in range(1, n_ctx):
            piece = jnp.where(my_ctx ^ mask == source, came[mask], piece)
        ordered.append(piece)
    w_wide = lax.all_gather(jnp.concatenate(ordered, axis=0), "dp", axis=0, tiled=True)

    def to_rows(gate, up):
        return lax.all_to_all(
            turn(gate, up, devices), BOTH, split_axis=0, concat_axis=0, tiled=True
        )

    length, second = lengths[0], doc_starts[0]
    places = my_ctx * span + jnp.arange(span, dtype=jnp.int32)
    doc_begin = jnp.where(places >= length, length, jnp.where(places >= second, second, 0))
    position = (places - doc_begin).astype(F32)
    live = (places < length)[:, None]
    info = jnp.stack([my_ctx, length, second]).astype(jnp.int32)
    inverse = ROPE_BASE ** (-2.0 * jnp.arange(HD // 2, dtype=F32) / HD)
    angles = inverse[:, None] * position[None, :]
    cosine, sine_part = jnp.cos(angles), jnp.sin(angles)
    cosine = jnp.concatenate([cosine, cosine], axis=0)[None]
    sine_part = jnp.concatenate([sine_part, sine_part], axis=0)[None]

    def from_ctx(value, other_x=None):
        other_core = swap(value, core_bit, devices)
        if other_x is None:
            other_x = swap(value, x_bit, devices)
        return value, other_core, other_x

    cot_here = jnp.where(live, cotangent.reshape(tokens, width), jnp.zeros((), BF16))

    def pair_of_heads(kv, index):
        begin = index * HD
        return jnp.concatenate(
            [kv[:, begin : begin + HD], kv[:, KVD + begin : KVD + begin + HD]], axis=1
        )

    inputs = block_input.astype(F32).reshape(tokens, width)
    scale_one = lax.rsqrt(jnp.mean(inputs * inputs, axis=-1, keepdims=True) + NORM_EPS)
    normed_one = (inputs * scale_one * gain_first).astype(BF16)
    bias = jnp.concatenate([bias_query, bias_key, bias_value])
    pre = mm(w_qkv, normed_one, ((0,), (1,))) + bias[:, None]
    turned = rotate(
        pre[: QD + KVD].reshape(HEADS + KVH, HD, tokens), cosine, sine_part
    )
    queries = (turned[:HEADS].astype(BF16).astype(F32) * HD ** (-0.5)).astype(BF16)
    kv_here = jnp.concatenate(
        [turned[HEADS:].astype(BF16).reshape(KVD, tokens), pre[QD + KVD :].astype(BF16)], axis=0
    )
    kv = from_ctx(kv_here)
    kv = jnp.stack(kv + (swap(kv[2], core_bit, devices),))
    back_one = jnp.pad(
        normed_one.T.reshape(devices, rows, tokens), ((0, 0), (0, padded - rows), (0, 0))
    ).reshape(devices * padded, tokens)
    back_one, kv = lax.optimization_barrier((back_one, kv))
    down_came = [down_part] + down_came
    at_z = jnp.where((me & high) != 0, 2, 0) + jnp.where((me & low) != 0, 1, 0)
    ordered = []
    for source in range(4):
        piece = down_came[0]
        for mask in range(1, 4):
            piece = jnp.where(at_z ^ mask == source, down_came[mask], piece)
        ordered.append(piece)
    down_part = jnp.stack(ordered).reshape(2, 2, frows, D)
    kv, down_part = lax.optimization_barrier((kv, down_part))
    down_came = swap(down_part, down_bits[2], devices)
    out_full, kv = lax.optimization_barrier((attn_full[..., qkv:], kv))
    halves = []
    for index in range(KVH):
        if index == 1:
            out_full, cot_here, halves = lax.optimization_barrier((out_full, cot_here, halves))
            cot_far = swap(cot_here, x_bit, devices)
        out_full = gather_bits(
            out_full, ctx_bits[::-1][index : index + 1], me, devices, dp_bits + ctx_bits[::-1][:index]
        )
        kv_one = pair_of_heads(kv, index)
        halves.append(attend(info, kv_one, queries[index * group : (index + 1) * group]))
    halves, cot_far, down_came = lax.optimization_barrier((halves, cot_far, down_came))
    down_part = jnp.where(
        (me & down_bits[2]) != 0,
        jnp.stack([down_came, down_part], axis=2),
        jnp.stack([down_part, down_came], axis=2),
    )
    down_part = gather_bits(down_part, down_bits[3:], me, devices, down_bits[:3])
    attended = jnp.concatenate([half[0] for half in halves], axis=0)
    log_total = jnp.concatenate([half[1] for half in halves], axis=0)
    out_pieces = out_full.reshape(devices * padded, D)

    mixed_pieces = jnp.pad(
        attended.reshape(devices, rows, tokens).astype(BF16), ((0, 0), (0, padded - rows), (0, 0))
    ).reshape(devices * padded, tokens)
    hidden = inputs + mm(mixed_pieces, out_pieces, ((0,), (0,)))
    scale_two = lax.rsqrt(jnp.mean(hidden * hidden, axis=-1, keepdims=True) + NORM_EPS)
    normed_two = (hidden * scale_two * gain_second).astype(BF16)

    normed_two, down_part = lax.optimization_barrier((normed_two, down_part))
    w_down = down_part.reshape(fblock, D)
    normed = from_ctx(normed_two)
    out_pieces, own = lax.optimization_barrier((out_pieces, normed[0]))
    normed = (own,) + normed[1:]
    w_out = out_pieces.reshape(devices, padded, D)[:, :rows].reshape(QD, D)
    cot = from_ctx(cot_here, cot_far)
    kept, near_parts = feed_forward(normed[:2], cot[:2], w_wide, w_down, n_ctx, None)
    (far_x, far_dy), momentum_flat, kept = lax.optimization_barrier(
        ((normed[2], cot[2]), momentum_flat, kept)
    )
    old_qkv, old_out, old_pair, old_down = pack(momentum_flat, None, devices, 1, F32)
    old_pair, far_x = lax.optimization_barrier((old_pair, far_x))
    old_pair = lax.all_to_all(old_pair, BOTH, split_axis=0, concat_axis=0, tiled=True)
    kept, far_parts = feed_forward(
        (far_x, swap(far_x, core_bit, devices)),
        (far_dy, swap(far_dy, core_bit, devices)),
        w_wide,
        w_down,
        n_ctx,
        kept,
    )
    kept, far_parts, old_pair = lax.optimization_barrier((kept, far_parts, old_pair))
    acts, both_backs, normed_all, cot_all = kept

    def to_ctx(near, far):
        crossed = swap(far[1], core_bit, devices)
        far = (far[0].astype(F32) + crossed.astype(F32)).astype(BF16)
        crossed = swap(near[1], core_bit, devices)
        near = near[0].astype(F32) + crossed.astype(F32)
        return near + swap(far, x_bit, devices).astype(F32), far

    normed_two_grad, ready = to_ctx(near_parts, far_parts)
    (acts, both_backs), ready = lax.optimization_barrier(((acts, both_backs), ready))

    dp_shape = tuple([2] * len(dp_bits)) + (frows, D)
    dp_order = dp_bits[1:] + dp_bits[:1]
    down_value = mm(acts, cot_all, ((0,), (0,))).astype(BF16)
    both_value = mm(both_backs, normed_all, ((0,), (0,))).astype(BF16)
    values = [both_value[:fblock], both_value[fblock:], down_value]
    orders = [dp_bits, dp_order, dp_bits]
    started = []
    for index in (2, 1, 0):
        sent, kept = scatter_split(values[index].reshape(dp_shape), dp_bits, orders[index][0], me)
        started.insert(0, (kept, swap(sent, orders[index][0], devices)))

    out_grad = cot_here.astype(F32)
    hidden_norm_grad, grad_gain_second = norm_backward(
        hidden, scale_two, gain_second, normed_two_grad
    )
    hidden_grad = out_grad + hidden_norm_grad
    hidden_low = hidden_grad.astype(BF16)
    heads_grad = mm(w_out, hidden_low, ((1,), (1,))).astype(BF16).reshape(HEADS, HD, tokens)
    delta = jnp.sum(heads_grad.astype(F32) * attended, axis=1, keepdims=True)
    grad_output = mm(mixed_pieces, hidden_low)
    query_grads, kv_parts = [], []
    sent, kept = scatter_split(
        grad_output.astype(BF16).reshape(many + (padded, D)), all_bits, all_bits[0], me
    )
    wide_parts = started + [(kept, swap(sent, all_bits[0], devices))]
    wide_orders = [list(order) for order in orders] + [list(all_bits)]
    steps = [[1, 0, 3], [2, 3], [1, 0, 3], [2, 3]]
    shares = [4, 3]
    ready = [sent]
    for index in range(KVH):
        kv_one = pair_of_heads(kv, index)
        kv_grad = None
        begin = index * group
        for count in shares:
            chosen = slice(begin, begin + count)
            begin += count
            query_part, ready = lax.optimization_barrier((queries[chosen], ready))
            query_grad, kv_grad = attend_back(
                info, kv_one, query_part, heads_grad[chosen], log_total[chosen], delta[chosen], kv_grad
            )
            query_grads.append(query_grad)
            ready = []
            if len(steps) == 3:
                acts, query_grads[-1] = lax.optimization_barrier((acts, query_grad))
                out_part = mm(acts, w_down).astype(BF16).reshape(n_ctx, span, D)
                out_near = (out_part[0], swap(out_part[1], core_bit, devices))
                out_far = scatter_end((out_part[2], swap(out_part[3], core_bit, devices)))
                ready.append(out_far)
            for which in steps.pop(0):
                order = wide_orders[which]
                parts, query_grads[-1] = lax.optimization_barrier(
                    (wide_parts[which], query_grads[-1])
                )
                order.pop(0)
                sent, kept = scatter_split(scatter_end(parts), order, order[0], me)
                ready.append(sent)
                wide_parts[which] = (kept, swap(sent, order[0], devices))
        kv_parts.append(
            scatter_sum(kv_grad.reshape(2, 2, 2 * HD, span), ctx_bits, me, devices)
        )
    kv_grads = [part.astype(F32).reshape(2, HD, span) for part in kv_parts]
    qk_grad = jnp.concatenate(query_grads + [grad[:1] for grad in kv_grads], axis=0)
    qk_back = rotate_back(qk_grad, cosine, sine_part).reshape(QD + KVD, tokens)
    qkv_back = jnp.concatenate(
        [qk_back] + [grad[1] for grad in kv_grads], axis=0
    ).astype(BF16)
    grad_qkv = mm(back_one, qkv_back, ((1,), (1,)))
    here_core = jnp.where((me & core_bit) != 0, 1, 0)
    here_x = jnp.where((me & x_bit) != 0, 1, 0)
    left = list(all_bits)
    qkv_order = [core_bit, dp_bits[0], x_bit] + dp_bits[1:]
    sent, kept = scatter_split(
        grad_qkv.astype(BF16).reshape(many + (padded, qkv)), left, core_bit, me
    )
    wide_parts, sent = lax.optimization_barrier((wide_parts, sent))
    qkv_parts = (kept, swap(sent, core_bit, devices))
    left.remove(core_bit)
    gate_sum, up_sum, down_sum, out_sum_rows = [
        scatter_sum(scatter_end(parts), order[1:], me, devices)
        for parts, order in zip(wide_parts, wide_orders)
    ]
    mats = combine(old_pair, gate_sum, up_sum, old_down, down_sum, old_out, out_sum_rows)
    mats = mats.reshape(2, 2, frows, D)
    row_parts = (choose(mats, here_core, 1), swap(choose(mats, 1 - here_core, 1), core_bit, devices))
    count = len(block_pairs(D // BLOCK))
    places = (count + n_dp - 1) // n_dp * n_dp
    dp_many = tuple([2] * len(dp_bits))
    gram_left = list(dp_bits)
    for step, bit in enumerate(qkv_order[1:]):
        qkv_parts, row_parts = lax.optimization_barrier((qkv_parts, row_parts))
        sent, kept = scatter_split(scatter_end(qkv_parts), left, bit, me)
        left.remove(bit)
        qkv_parts = (kept, swap(sent, bit, devices))
        if step == 0:
            mats = jnp.stack(row_parts, axis=1)
            row_parts = (choose(mats, here_x, 0), swap(choose(mats, 1 - here_x, 0), x_bit, devices))
            continue
        if step == 1:
            owned = jnp.stack(row_parts).reshape(n_ctx * frows, D)
            gram = gram_blocks(owned, places).reshape(dp_many + (places // n_dp, BLOCK, BLOCK))
        else:
            gram = scatter_end(row_parts)
        sent, kept = scatter_split(gram, gram_left, gram_left[0], me)
        row_parts = (kept, swap(sent, gram_left.pop(0), devices))
    qkv_parts, row_parts, out_far = lax.optimization_barrier((qkv_parts, row_parts, out_far))
    out_far = swap(out_far, x_bit, devices)
    qkv_sum_rows = scatter_end(qkv_parts)
    moved_qkv = MOMENTUM_DECAY * old_qkv + qkv_sum_rows.astype(F32)
    moved_low = moved_qkv.astype(BF16)
    qkv_all = lax.all_gather(moved_low, BOTH, axis=0, tiled=True)
    gram = gather_bits(scatter_end(row_parts), dp_bits[::-1], me, devices)
    gram = gram.reshape(places, BLOCK, BLOCK)

    (gate_sum, up_sum), out_far, gram = lax.optimization_barrier(
        ((gate_sum, up_sum), out_far, gram)
    )
    out_sum = out_near[0].astype(F32) + out_near[1].astype(F32) + out_far.astype(F32)
    layer_out = jnp.where(live, hidden + out_sum, 0.0).astype(BF16)
    pair_rows = to_rows(gate_sum, up_sum)
    ortho = orthogonal_wide(gram, owned).reshape(2, 2, frows, D)
    ortho, pair_rows = lax.optimization_barrier((ortho, pair_rows))
    got = swap(ortho[1], x_bit, devices)
    qkv_back, own = lax.optimization_barrier((qkv_back, ortho[0]))
    grad_bias = jnp.sum(qkv_back.astype(F32), axis=1)
    normed_one_grad = mm(qkv_back, w_qkv, ((0,), (1,)))
    input_norm_grad, grad_gain_first = norm_backward(inputs, scale_one, gain_first, normed_one_grad)
    input_grad = (hidden_grad + input_norm_grad).astype(BF16).reshape(slots, span, width)

    vector_part = join_small(
        [
            grad_gain_first,
            grad_gain_second,
            grad_bias[:QD],
            grad_bias[QD : QD + KVD],
            grad_bias[QD + KVD :],
        ],
        devices,
    )
    vector_rows = lax.all_to_all(vector_part, BOTH, split_axis=0, concat_axis=0, tiled=True)
    own, vector_part = lax.optimization_barrier((own, vector_part))
    ortho = jnp.where((me & x_bit) != 0, jnp.stack([got, own]), jnp.stack([own, got]))
    got = swap(ortho[:, 1], core_bit, devices)
    ortho = jnp.where(
        (me & core_bit) != 0,
        jnp.stack([got, ortho[:, 0]], axis=1),
        jnp.stack([ortho[:, 0], got], axis=1),
    ).reshape(n_ctx, frows, D)
    turned = turn(ortho[0], ortho[1], devices)
    momentum_flat, turned = lax.optimization_barrier((momentum_flat, turned))
    ortho_pair = lax.all_to_all(turned, BOTH, split_axis=0, concat_axis=0, tiled=True)
    ortho_qkv = orthogonal_whole(qkv_all, moved_qkv, (QD, KVD, KVD))
    vector_rows, ortho_qkv = lax.optimization_barrier((vector_rows, ortho_qkv))
    new_momentum = update(
        momentum_flat,
        qkv_sum_rows,
        out_sum_rows,
        pair_rows,
        down_sum,
        devices,
        MOMENTUM_DECAY,
        [1.0] * 7,
    ).reshape(momentum.shape)

    factors = [
        -MUON_RATE * math.sqrt(max(1.0, breadth / height)) for height, breadth in matrix_shapes()
    ]
    new_master = update(
        master_flat,
        ortho_qkv,
        ortho[3, :padded],
        ortho_pair,
        ortho[2],
        devices,
        1.0 - MUON_RATE * MUON_DECAY,
        factors,
    ).reshape(master.shape)
    vector_grad = jnp.sum(vector_rows, axis=0, keepdims=True)
    first_new = BETA_FIRST * vector_first + (1.0 - BETA_FIRST) * vector_grad
    second_new = BETA_SECOND * vector_second + (1.0 - BETA_SECOND) * vector_grad * vector_grad
    adjusted = (
        first_new
        / (1.0 - BETA_FIRST**STEP)
        / (jnp.sqrt(second_new / (1.0 - BETA_SECOND**STEP)) + ADAM_EPS)
    )
    new_vectors = vectors - ADAM_RATE * adjusted
    return (
        layer_out.reshape(slots, span, width),
        input_grad,
        new_master,
        new_momentum,
        new_master.astype(BF16),
        new_vectors,
        first_new,
        second_new,
    )


def solution(mesh):
    return jax.shard_map(
        on_device,
        mesh=mesh,
        in_specs=(
            P("dp", "ctx", None),
            P("dp", "ctx", None),
            P("dp"),
            P("dp"),
            P(BOTH, None),
            P(BOTH, None),
            P(BOTH, None),
            P(BOTH, None),
            P(BOTH, None),
        ),
        out_specs=(
            P("dp", "ctx", None),
            P("dp", "ctx", None),
            P(BOTH, None),
            P(BOTH, None),
            P(BOTH, None),
            P(BOTH, None),
            P(BOTH, None),
            P(BOTH, None),
        ),
        check_vma=False,
    )
```

profile of v0, /device:TPU:0, one launch (start us, length us, event | category | flops | bytes accessed | tf_op | source)
XLA Modules:
  0.0 548.6 jit_solution(17595237591235902327)
XLA Ops:
  21.4 6.7 %collective-permute-done.4 = bf16[2,32,2048]{2,1,0:T(8,128)(2,1)S(1)} collective-permute-done((bf16[2,32,2048]{2,1,0:T(8,128)(2,1)S(1)}, bf16[2,32,2048]{2,1,0:T(8,128)(2,1)S(1)}, u32[]{:S(2)}, u32[]{:S(2)}) %collective-permute-start.4) | collective-permute-done | bytes 262176 | tf_op jit(solution)/shard_map/ppermute | solution.py:68
  30.0 10.5 %collective-permute-done.5 = bf16[2,2,32,2048]{3,2,0,1:T(8,128)(2,1)S(1)} collective-permute-done((bf16[2,2,32,2048]{3,2,0,1:T(8,128)(2,1)S(1)}, bf16[2,2,32,2048]{3,2,0,1:T(8,128)(2,1)S(1)}, u32[]{:S(2)}, u32[]{:S(2)}) %collective-permute-start.5) | collective-permute-done | bytes 524320 | tf_op jit(solution)/shard_map/ppermute | solution.py:68
  60.3 9.9 %collective-permute-done.12 = bf16[152,896]{1,0:T(8,128)(2,1)} collective-permute-done((bf16[152,896]{1,0:T(8,128)(2,1)S(1)}, bf16[152,896]{1,0:T(8,128)(2,1)}, u32[]{:S(2)}, u32[]{:S(2)}) %collective-permute-start.12) | collective-permute-done | bytes 272416 | tf_op jit(solution)/shard_map/ppermute | solution.py:68
  85.8 7.3 %collective-permute-done.9 = bf16[256,512]{1,0:T(8,128)(2,1)} collective-permute-done((bf16[256,512]{1,0:T(8,128)(2,1)}, bf16[256,512]{1,0:T(8,128)(2,1)}, u32[]{:S(2)}, u32[]{:S(2)}) %collective-permute-start.9) | collective-permute-done | bytes 262176 | tf_op jit(solution)/shard_map/ppermute | solution.py:68
  106.0 6.2 %collective-permute-done.14 = bf16[2,2,2,32,896]{4,3,0,2,1:T(8,128)(2,1)S(1)} collective-permute-done((bf16[2,2,2,32,896]{4,3,0,2,1:T(8,128)(2,1)S(1)}, bf16[2,2,2,32,896]{4,3,0,2,1:T(8,128)(2,1)S(1)}, u32[]{:S(2)}, u32[]{:S(2)}) %collective-permute-start.14) | collective-permute-done | bytes 458784 | tf_op jit(solution)/shard_map/ppermute | solution.py:68
  115.0 9.5 %collective-permute-start.15 = (bf16[512,896]{1,0:T(8,128)(2,1)}, bf16[512,896]{1,0:T(8,128)(2,1)S(1)}, u32[]{:S(2)}, u32[]{:S(2)}) collective-permute-start(bf16[512,896]{1,0:T(8,128)(2,1)} %bitcast_select_fusion.dy0), channel_id=1, source_target_pairs={{0,2},{1,3},{2,0},{3,1},{4,6},{5,7},{6,4},{7,5},{8,10},{9,11},{10,... | collective-permute-start | bytes 2752520 | tf_op jit(solution)/shard_map/ppermute | solution.py:68
  137.9 9.4 %collective-permute-done.16 = bf16[2,2,152,896]{3,2,1,0:T(8,128)(2,1)} collective-permute-done((bf16[2,2,152,896]{3,2,1,0:T(8,128)(2,1)}, bf16[2,2,152,896]{3,2,1,0:T(8,128)(2,1)}, u32[]{:S(2)}, u32[]{:S(2)}) %collective-permute-start.16) | collective-permute-done | bytes 1089568 | tf_op jit(solution)/shard_map/ppermute | solution.py:68
  164.3 22.0 %feed_forward.2 = (bf16[2048,1216]{1,0:T(8,128)(2,1)}, bf16[2048,2432]{1,0:T(8,128)(2,1)}, bf16[2048,896]{1,0:T(8,128)(2,1)}, bf16[2048,896]{1,0:T(8,128)(2,1)},...) custom-call(bf16[512,896]{1,0:T(8,128)(2,1)} %multiply_convert_fusion.x0, ...), custom_call_target="tpu_custom_call" | custom-call | flops 11156848640 | bytes 15712256 | tf_op jit(solution)/shard_map/feed_forward/pallas_call | solution.py:377
  188.3 7.1 %all-to-all-start = ((bf16[32,28,304]{2,1,0:T(8,128)(2,1)}), bf16[32,28,304]{2,1,0:T(8,128)(2,1)S(1)}, u32[]{:S(2)}, u32[]{:S(2)}) async-start(bf16[32,28,304]{2,1,0:T(8,128)(2,1)} %get-tuple-element.214), calls=%async_computation | async-start | bytes 1572864 | tf_op jit(solution)/shard_map/all_to_all | solution.py:881
  195.4 22.2 %feed_forward.3 = (bf16[2048,1216]{1,0:T(8,128)(2,1)}, bf16[2048,2432]{1,0:T(8,128)(2,1)}, bf16[2048,896]{1,0:T(8,128)(2,1)}, bf16[2048,896]{1,0:T(8,128)(2,1)},...) custom-call(bf16[512,896]{1,0:T(8,128)(2,1)} %collective-permute-don, ...), custom_call_target="tpu_custom_call", output_to_operand_aliasing={{0}: (6, {}), {1}: (7, {}), {2}: (8, {}), {3}: (9, {})} | custom-call | flops 11156848640 | bytes 15712256 | tf_op jit(solution)/shard_map/feed_forward/pallas_call | solution.py:377
  228.1 15.2 %convolution_convert_fusion = bf16[2432,896]{1,0:T(8,128)(2,1)S(1)} fusion(bf16[2048,2432]{1,0:T(8,128)(2,1)} %get-tuple-element.220, bf16[2048,896]{1,0:T(8,128)(2,1)} %get-tuple-element.221), kind=kOutput, calls=%fused_computation | convolution fusion | flops 8927657984 | bytes 17989632 | tf_op jit(solution)/shard_map/dot_general | solution.py:50
  275.0 7.1 %collective-permute-start.34 = (bf16[2,2,2,32,896]{4,3,2,1,0:T(8,128)(2,1)S(1)}, bf16[2,2,2,32,896]{4,3,2,1,0:T(8,128)(2,1)S(1)}, u32[]{:S(2)}, u32[]{:S(2)}) collective-permute-start(bf16[2,2,2,32,896]{4,3,2,1,0:T(8,128)(2,1)S(1)} %get-tuple-element.387), channel_id=1, source_target_pairs={{0,2},{1,3},{2,0},{3,1},{4,6},{5,7},{6,4},{7,5},{8,10},{9,11},{10,... | collective-permute-start | bytes 1376264 | tf_op jit(solution)/shard_map/ppermute | solution.py:68
  286.6 5.8 %collective-permute-start.42 = (bf16[2,128,512]{2,1,0:T(8,128)(2,1)S(1)}, bf16[2,128,512]{2,1,0:T(8,128)(2,1)S(1)}, u32[]{:S(2)}, u32[]{:S(2)}) collective-permute-start(bf16[2,128,512]{2,1,0:T(8,128)(2,1)S(1)} %dynamic-slice_bitcast_fusion.31), channel_id=1, source_target_pairs={{0,1},{1,0},{2,3},{3,2},{4,5},{5,4},{6,7},{7,6},{8,9},{9,8},{10,11... | collective-permute-start | bytes 786440 | tf_op jit(solution)/shard_map/ppermute | solution.py:68
  299.9 6.2 %collective-permute-start.43 = (bf16[128,512]{1,0:T(8,128)(2,1)S(1)}, bf16[128,512]{1,0:T(8,128)(2,1)S(1)}, u32[]{:S(2)}, u32[]{:S(2)}) collective-permute-start(bf16[128,512]{1,0:T(8,128)(2,1)S(1)} %dynamic-slice_bitcast_fusion.43), channel_id=1, source_target_pairs={{0,2},{1,3},{2,0},{3,1},{4,6},{5,7},{6,4},{7,5},{8,10},{9,11},{10,... | collective-permute-start | bytes 393224 | tf_op jit(solution)/shard_map/ppermute | solution.py:68
  335.2 13.9 %collective-permute-start.45 = (bf16[128,512]{1,0:T(8,128)(2,1)S(1)}, bf16[128,512]{1,0:T(8,128)(2,1)S(1)}, u32[]{:S(2)}, u32[]{:S(2)}) collective-permute-start(bf16[128,512]{1,0:T(8,128)(2,1)S(1)} %dynamic-slice_bitcast_fusion.42), channel_id=1, source_target_pairs={{0,2},{1,3},{2,0},{3,1},{4,6},{5,7},{6,4},{7,5},{8,10},{9,11},{10,... | collective-permute-start | bytes 393224 | tf_op jit(solution)/shard_map/ppermute | solution.py:68
  361.8 6.8 %collective-permute-start.49 = (bf16[2,152,896]{2,1,0:T(8,128)(2,1)S(1)}, bf16[2,152,896]{2,1,0:T(8,128)(2,1)S(1)}, u32[]{:S(2)}, u32[]{:S(2)}) collective-permute-start(bf16[2,152,896]{2,1,0:T(8,128)(2,1)S(1)} %get-tuple-element.357), channel_id=1, source_target_pairs={{0,2},{1,3},{2,0},{3,1},{4,6},{5,7},{6,4},{7,5},{8,10},{9,11},{10,... | collective-permute-start | bytes 1634312 | tf_op jit(solution)/shard_map/ppermute | solution.py:68
  368.6 12.4 %collective-permute-done.49 = bf16[2,152,896]{2,1,0:T(8,128)(2,1)S(1)} collective-permute-done((bf16[2,152,896]{2,1,0:T(8,128)(2,1)S(1)}, bf16[2,152,896]{2,1,0:T(8,128)(2,1)S(1)}, u32[]{:S(2)}, u32[]{:S(2)}) %collective-permute-start.49) | collective-permute-done | bytes 544800 | tf_op jit(solution)/shard_map/ppermute | solution.py:68
  385.6 6.2 %collective-permute-done.50 = bf16[2,2,32,1152]{3,2,1,0:T(8,128)(2,1)S(1)} collective-permute-done((bf16[2,2,32,1152]{3,2,1,0:T(8,128)(2,1)S(1)}, bf16[2,2,32,1152]{3,2,1,0:T(8,128)(2,1)S(1)}, u32[]{:S(2)}, u32[]{:S(2)}) %collective-permute-start.50) | collective-permute-done | bytes 294944 | tf_op jit(solution)/shard_map/ppermute | solution.py:68
  397.9 7.5 %collective-permute-done.52 = bf16[2,32,1152]{2,1,0:T(8,128)(2,1)S(1)} collective-permute-done((bf16[2,32,1152]{2,1,0:T(8,128)(2,1)S(1)}, bf16[2,32,1152]{2,1,0:T(8,128)(2,1)S(1)}, u32[]{:S(2)}, u32[]{:S(2)}) %collective-permute-start.52) | collective-permute-done | bytes 147488 | tf_op jit(solution)/shard_map/ppermute | solution.py:68
  408.7 6.7 %collective-permute-done.54 = bf16[32,1152]{1,0:T(8,128)(2,1)S(1)} collective-permute-done((bf16[32,1152]{1,0:T(8,128)(2,1)S(1)}, bf16[32,1152]{1,0:T(8,128)(2,1)S(1)}, u32[]{:S(2)}, u32[]{:S(2)}) %collective-permute-start.54) | collective-permute-done | bytes 73760 | tf_op jit(solution)/shard_map/ppermute | solution.py:68
  416.1 7.2 %collective-permute-done.57 = bf16[4,128,128]{2,1,0:T(8,128)(2,1)S(1)} collective-permute-done((bf16[4,128,128]{2,1,0:T(8,128)(2,1)S(1)}, bf16[4,128,128]{2,1,0:T(8,128)(2,1)S(1)}, u32[]{:S(2)}, u32[]{:S(2)}) %collective-permute-start.57) | collective-permute-done | bytes 131104 | tf_op jit(solution)/shard_map/ppermute | solution.py:68
  458.7 17.8 %newton_wide.1 = bf16[608,896]{1,0:T(8,128)(2,1)S(1)} custom-call(bf16[32,128,128]{2,1,0:T(8,128)(2,1)S(1)} %bitcast.363, bf16[608,896]{1,0:T(8,128)(2,1)S(1)} %bitcast.359), custom_call_target="tpu_custom_call" | custom-call | flops 10070523904 | bytes 2179072 | tf_op jit(solution)/shard_map/newton_wide/pallas_call | solution.py:482
  491.3 7.4 %collective-permute-done.60 = bf16[2,152,896]{2,1,0:T(8,128)(2,1)S(1)} collective-permute-done((bf16[2,152,896]{2,1,0:T(8,128)(2,1)}, bf16[2,152,896]{2,1,0:T(8,128)(2,1)S(1)}, u32[]{:S(2)}, u32[]{:S(2)}) %collective-permute-start.60) | collective-permute-done | bytes 544800 | tf_op jit(solution)/shard_map/ppermute | solution.py:68
  514.4 19.9 %newton_whole.1.refs_1_ = bf16[32,1152]{1,0:T(8,128)(2,1)S(1)} custom-call(bf16[1024,1152]{1,0:T(8,128)(2,1)S(1)} %copy-done.10, f32[32,1152]{1,0:T(8,128)S(1)} %get-tuple-element.328.refs_1_), custom_call_target="tpu_custom_call" | custom-call | flops 11576279040 | bytes 2359296 | tf_op jit(solution)/shard_map/newton_whole/pallas_call | solution.py:515
  (463 shorter events, 280.1 us)
Async XLA Ops:
  7.2 157.1 %all-gather.3.cloned.1.call-start = ((), (), s32[]{:S(2)}) async-start(), calls=%async_computation.4 | async-start | bytes 4902912 | tf_op jit(solution)/shard_map/all_gather | solution.py:777
  15.0 32.6 %collective-permute-start.2 = (bf16[28,2432]{1,0:T(8,128)(2,1)}, bf16[28,2432]{1,0:T(8,128)(2,1)}, u32[]{:S(2)}, u32[]{:S(2)}) collective-permute-start(bf16[28,2432]{1,0:T(8,128)(2,1)} %get-tuple-element.396), channel_id=1, source_target_pairs={{0,3},{1,2},{2,1},{3,0},{4,7},{5,6},{6,5},{7,4},{8,11},{9,10},{10,... | collective-permute-start | bytes 408584 | tf_op jit(solution)/shard_map/ppermute | solution.py:68
  15.7 35.4 %collective-permute-start.1 = (bf16[28,2432]{1,0:T(8,128)(2,1)}, bf16[28,2432]{1,0:T(8,128)(2,1)}, u32[]{:S(2)}, u32[]{:S(2)}) collective-permute-start(bf16[28,2432]{1,0:T(8,128)(2,1)} %get-tuple-element.397), channel_id=1, source_target_pairs={{0,2},{1,3},{2,0},{3,1},{4,6},{5,7},{6,4},{7,5},{8,10},{9,11},{10,... | collective-permute-start | bytes 408584 | tf_op jit(solution)/shard_map/ppermute | solution.py:68
  16.5 34.6 %collective-permute-start = (bf16[28,2432]{1,0:T(8,128)(2,1)}, bf16[28,2432]{1,0:T(8,128)(2,1)}, u32[]{:S(2)}, u32[]{:S(2)}) collective-permute-start(bf16[28,2432]{1,0:T(8,128)(2,1)} %get-tuple-element.398), channel_id=1, source_target_pairs={{0,1},{1,0},{2,3},{3,2},{4,5},{5,4},{6,7},{7,6},{8,9},{9,8},{10,11... | collective-permute-start | bytes 408584 | tf_op jit(solution)/shard_map/ppermute | solution.py:68
  113.3 34.1 %collective-permute-start.16 = (bf16[2,2,152,896]{3,2,1,0:T(8,128)(2,1)}, bf16[2,2,152,896]{3,2,1,0:T(8,128)(2,1)}, u32[]{:S(2)}, u32[]{:S(2)}) collective-permute-start(bf16[2,2,152,896]{3,2,1,0:T(8,128)(2,1)} %bitcast.37), channel_id=1, source_target_pairs={{0,4},{1,5},{2,6},{3,7},{4,0},{5,1},{6,2},{7,3},{8,12},{9,13},{10,... | collective-permute-start | bytes 3268616 | tf_op jit(solution)/shard_map/ppermute | solution.py:68
  115.0 32.4 %collective-permute-start.15 = (bf16[512,896]{1,0:T(8,128)(2,1)}, bf16[512,896]{1,0:T(8,128)(2,1)S(1)}, u32[]{:S(2)}, u32[]{:S(2)}) collective-permute-start(bf16[512,896]{1,0:T(8,128)(2,1)} %bitcast_select_fusion.dy0), channel_id=1, source_target_pairs={{0,2},{1,3},{2,0},{3,1},{4,6},{5,7},{6,4},{7,5},{8,10},{9,11},{10,... | collective-permute-start | bytes 2752520 | tf_op jit(solution)/shard_map/ppermute | solution.py:68
  130.0 33.1 %collective-permute-start.20 = (bf16[512,896]{1,0:T(8,128)(2,1)}, bf16[512,896]{1,0:T(8,128)(2,1)}, u32[]{:S(2)}, u32[]{:S(2)}) collective-permute-start(bf16[512,896]{1,0:T(8,128)(2,1)} %bitcast_select_fusion.dy0), channel_id=1, source_target_pairs={{0,1},{1,0},{2,3},{3,2},{4,5},{5,4},{6,7},{7,6},{8,9},{9,8},{10,11... | collective-permute-start | bytes 2752520 | tf_op jit(solution)/shard_map/ppermute | solution.py:68
  161.5 24.9 %collective-permute-start.18 = (bf16[512,896]{1,0:T(8,128)(2,1)}, bf16[512,896]{1,0:T(8,128)(2,1)}, u32[]{:S(2)}, u32[]{:S(2)}) collective-permute-start(bf16[512,896]{1,0:T(8,128)(2,1)} %multiply_convert_fusion.x0), channel_id=1, source_target_pairs={{0,2},{1,3},{2,0},{3,1},{4,6},{5,7},{6,4},{7,5},{8,10},{9,11},{10,... | collective-permute-start | bytes 2752520 | tf_op jit(solution)/shard_map/ppermute | solution.py:68
  188.3 29.3 %all-to-all-start = ((bf16[32,28,304]{2,1,0:T(8,128)(2,1)}), bf16[32,28,304]{2,1,0:T(8,128)(2,1)S(1)}, u32[]{:S(2)}, u32[]{:S(2)}) async-start(bf16[32,28,304]{2,1,0:T(8,128)(2,1)} %get-tuple-element.214), calls=%async_computation | async-start | bytes 1572864 | tf_op jit(solution)/shard_map/all_to_all | solution.py:881
  195.3 317.4 %all-gather.5.cloned.1.call-start = ((), (), s32[]{:S(2)}) async-start(), calls=%async_computation.5 | async-start | bytes 2433024 | tf_op jit(solution)/shard_map/all_gather | solution.py:1012
  224.3 30.6 %collective-permute-start.25 = (bf16[512,896]{1,0:T(8,128)(2,1)}, bf16[512,896]{1,0:T(8,128)(2,1)S(1)}, u32[]{:S(2)}, u32[]{:S(2)}) collective-permute-start(bf16[512,896]{1,0:T(8,128)(2,1)} %get-tuple-element.223), channel_id=1, source_target_pairs={{0,1},{1,0},{2,3},{3,2},{4,5},{5,4},{6,7},{7,6},{8,9},{9,8},{10,11... | collective-permute-start | bytes 2752520 | tf_op jit(solution)/shard_map/ppermute | solution.py:68
  226.3 28.6 %collective-permute-start.26 = (bf16[512,896]{1,0:T(8,128)(2,1)S(1)}, bf16[512,896]{1,0:T(8,128)(2,1)S(1)}, u32[]{:S(2)}, u32[]{:S(2)}) collective-permute-start(bf16[512,896]{1,0:T(8,128)(2,1)S(1)} %add_convert_fusion.6), channel_id=1, source_target_pairs={{0,2},{1,3},{2,0},{3,1},{4,6},{5,7},{6,4},{7,5},{8,10},{9,11},{10,... | collective-permute-start | bytes 2752520 | tf_op jit(solution)/shard_map/ppermute | solution.py:68
  243.9 25.9 %collective-permute-start.24 = (bf16[2,2,152,896]{3,2,1,0:T(8,128)(2,1)S(1)}, bf16[2,2,152,896]{3,2,1,0:T(8,128)(2,1)S(1)}, u32[]{:S(2)}, u32[]{:S(2)}) collective-permute-start(bf16[2,2,152,896]{3,2,1,0:T(8,128)(2,1)S(1)} %get-tuple-element.338), channel_id=1, source_target_pairs={{0,8},{1,9},{2,10},{3,11},{4,12},{5,13},{6,14},{7,15},{8,0},{9,1},... | collective-permute-start | bytes 3268616 | tf_op jit(solution)/shard_map/ppermute | solution.py:68
  245.7 27.0 %collective-permute-start.27 = (bf16[2,2,152,896]{3,2,1,0:T(8,128)(2,1)S(1)}, bf16[2,2,152,896]{3,2,1,0:T(8,128)(2,1)S(1)}, u32[]{:S(2)}, u32[]{:S(2)}) collective-permute-start(bf16[2,2,152,896]{3,2,1,0:T(8,128)(2,1)S(1)} %get-tuple-element.340), channel_id=1, source_target_pairs={{0,4},{1,5},{2,6},{3,7},{4,0},{5,1},{6,2},{7,3},{8,12},{9,13},{10,... | collective-permute-start | bytes 3268616 | tf_op jit(solution)/shard_map/ppermute | solution.py:68
  253.4 44.9 %collective-permute-start.33 = (bf16[2,2,152,896]{3,2,1,0:T(8,128)(2,1)S(1)}, bf16[2,2,152,896]{3,2,1,0:T(8,128)(2,1)S(1)}, u32[]{:S(2)}, u32[]{:S(2)}) collective-permute-start(bf16[2,2,152,896]{3,2,1,0:T(8,128)(2,1)S(1)} %get-tuple-element.336), channel_id=1, source_target_pairs={{0,4},{1,5},{2,6},{3,7},{4,0},{5,1},{6,2},{7,3},{8,12},{9,13},{10,... | collective-permute-start | bytes 3268616 | tf_op jit(solution)/shard_map/ppermute | solution.py:68
  270.2 48.4 %collective-permute-start.31 = (bf16[2,152,896]{2,1,0:T(8,128)(2,1)S(1)}, bf16[2,152,896]{2,1,0:T(8,128)(2,1)S(1)}, u32[]{:S(2)}, u32[]{:S(2)}) collective-permute-start(bf16[2,152,896]{2,1,0:T(8,128)(2,1)S(1)} %get-tuple-element.363), channel_id=1, source_target_pairs={{0,16},{1,17},{2,18},{3,19},{4,20},{5,21},{6,22},{7,23},{8,24},{9,... | collective-permute-start | bytes 1634312 | tf_op jit(solution)/shard_map/ppermute | solution.py:68
  273.2 45.5 %collective-permute-start.30 = (bf16[2,152,896]{2,1,0:T(8,128)(2,1)S(1)}, bf16[2,152,896]{2,1,0:T(8,128)(2,1)S(1)}, u32[]{:S(2)}, u32[]{:S(2)}) collective-permute-start(bf16[2,152,896]{2,1,0:T(8,128)(2,1)S(1)} %get-tuple-element.365), channel_id=1, source_target_pairs={{0,8},{1,9},{2,10},{3,11},{4,12},{5,13},{6,14},{7,15},{8,0},{9,1},... | collective-permute-start | bytes 1634312 | tf_op jit(solution)/shard_map/ppermute | solution.py:68
  275.0 36.2 %collective-permute-start.34 = (bf16[2,2,2,32,896]{4,3,2,1,0:T(8,128)(2,1)S(1)}, bf16[2,2,2,32,896]{4,3,2,1,0:T(8,128)(2,1)S(1)}, u32[]{:S(2)}, u32[]{:S(2)}) collective-permute-start(bf16[2,2,2,32,896]{4,3,2,1,0:T(8,128)(2,1)S(1)} %get-tuple-element.387), channel_id=1, source_target_pairs={{0,2},{1,3},{2,0},{3,1},{4,6},{5,7},{6,4},{7,5},{8,10},{9,11},{10,... | collective-permute-start | bytes 1376264 | tf_op jit(solution)/shard_map/ppermute | solution.py:68
  320.1 36.6 %collective-permute-start.35 = (bf16[152,896]{1,0:T(8,128)(2,1)S(1)}, bf16[152,896]{1,0:T(8,128)(2,1)S(1)}, u32[]{:S(2)}, u32[]{:S(2)}) collective-permute-start(bf16[152,896]{1,0:T(8,128)(2,1)S(1)} %get-tuple-element.406), channel_id=1, source_target_pairs={{0,16},{1,17},{2,18},{3,19},{4,20},{5,21},{6,22},{7,23},{8,24},{9,... | collective-permute-start | bytes 817160 | tf_op jit(solution)/shard_map/ppermute | solution.py:68
  320.8 35.9 %collective-permute-start.36 = (bf16[152,896]{1,0:T(8,128)(2,1)S(1)}, bf16[152,896]{1,0:T(8,128)(2,1)S(1)}, u32[]{:S(2)}, u32[]{:S(2)}) collective-permute-start(bf16[152,896]{1,0:T(8,128)(2,1)S(1)} %get-tuple-element.404), channel_id=1, source_target_pairs={{0,4},{1,5},{2,6},{3,7},{4,0},{5,1},{6,2},{7,3},{8,12},{9,13},{10,... | collective-permute-start | bytes 817160 | tf_op jit(solution)/shard_map/ppermute | solution.py:68
  331.9 24.8 %collective-permute-start.39 = (bf16[152,896]{1,0:T(8,128)(2,1)S(1)}, bf16[152,896]{1,0:T(8,128)(2,1)S(1)}, u32[]{:S(2)}, u32[]{:S(2)}) collective-permute-start(bf16[152,896]{1,0:T(8,128)(2,1)S(1)} %get-tuple-element.402), channel_id=1, source_target_pairs={{0,16},{1,17},{2,18},{3,19},{4,20},{5,21},{6,22},{7,23},{8,24},{9,... | collective-permute-start | bytes 817160 | tf_op jit(solution)/shard_map/ppermute | solution.py:68
  424.8 30.1 %collective-permute-start.29 = (bf16[512,896]{1,0:T(8,128)(2,1)}, bf16[512,896]{1,0:T(8,128)(2,1)}, u32[]{:S(2)}, u32[]{:S(2)}) collective-permute-start(bf16[512,896]{1,0:T(8,128)(2,1)} %get-tuple-element.332), channel_id=1, source_target_pairs={{0,1},{1,0},{2,3},{3,2},{4,5},{5,4},{6,7},{7,6},{8,9},{9,8},{10,11... | collective-permute-start | bytes 2752520 | tf_op jit(solution)/shard_map/ppermute | solution.py:68
  449.5 29.1 %all-to-all-start.1 = ((bf16[32,28,304]{2,1,0:T(8,128)(2,1)}), bf16[32,28,304]{2,1,0:T(8,128)(2,1)S(1)}, u32[]{:S(2)}, u32[]{:S(2)}) async-start(bf16[32,28,304]{2,1,0:T(8,128)(2,1)} %turn.2), calls=%async_computation.1 | async-start | bytes 1572864 | tf_op jit(solution)/shard_map/all_to_all | solution.py:780
  507.8 26.5 %all-to-all-start.3 = ((bf16[32,28,304]{2,1,0:T(8,128)(2,1)}), bf16[32,28,304]{2,1,0:T(8,128)(2,1)S(1)}, u32[]{:S(2)}, u32[]{:S(2)}) async-start(bf16[32,28,304]{2,1,0:T(8,128)(2,1)} %turn.3), calls=%async_computation.3 | async-start | bytes 1572864 | tf_op jit(solution)/shard_map/all_to_all | solution.py:1052
  (110 other events, 1133.6 us)
Sparse Core Ops, SparseCore 0:
  60.4 83.4 all-gather.2
  436.3 62.6 all-gather.4
where the time goes:
time: 554 us; the launch traced here: 549 us
  starting transfers between devices  132 us (24%)
  waiting for transfers between devices  128 us (23%)
  Pallas kernels  123 us (22%)
  other arithmetic  64.5 us (12%)
  local copies, waits for them, and re-layouts  42.8 us (8%)
  matrix products  40.9 us (7%)
  between operations  17.6 us (3%)
    ppermute x62, waiting for transfers between devices, swap(): lax.ppermute(value, BOTH, [(index, index ^ mask) for index in range(devic...  126 us
    ppermute x62, starting transfers between devices, swap(): lax.ppermute(value, BOTH, [(index, index ^ mask) for index in range(devic...  111 us
    pallas_call x2, Pallas kernels, feed_forward(): pl.pallas_call(body, grid=(2,), in_specs=in_specs, out_specs=[line(count)...  44.2 us
    dot_general x9, matrix products, mm(): lax.dot_general(left, right, (contract, ((), ())), preferred_element_type...  40.9 us
    pallas_call x1, Pallas kernels, orthogonal_whole(): pl.pallas_call(lambda *refs: whole_kernel(widths, *refs), out_shape=jax.S...  19.9 us
    pallas_call x4, Pallas kernels, attend_back(): pl.pallas_call(body, grid=(heads,), in_specs=[pl.BlockSpec(memory_space=p...  19.8 us
    pallas_call x1, Pallas kernels, orthogonal_wide(): pl.pallas_call(wide_kernel, out_shape=jax.ShapeDtypeStruct(rows.shape, BF...  17.8 us
    select_n x15, other arithmetic, gather_bits(): jnp.where(mine, jnp.stack([got, held], axis=place), jnp.stack([held, got]...  14.5 us
  transfers between devices with their start and end apart: 68, of which 25 were waited for; matrix products, arithmetic and copies ran while one was open for 23% of the time, Pallas kernels for 22%

commit v1 on v0

--- a/solution.py
+++ b/solution.py
@@ -1013,16 +1013,14 @@
     gram = gather_bits(scatter_end(row_parts), dp_bits[::-1], me, devices)
     gram = gram.reshape(places, BLOCK, BLOCK)
 
-    (gate_sum, up_sum), out_far, gram = lax.optimization_barrier(
-        ((gate_sum, up_sum), out_far, gram)
-    )
-    out_sum = out_near[0].astype(F32) + out_near[1].astype(F32) + out_far.astype(F32)
-    layer_out = jnp.where(live, hidden + out_sum, 0.0).astype(BF16)
+    (gate_sum, up_sum), gram = lax.optimization_barrier(((gate_sum, up_sum), gram))
     pair_rows = to_rows(gate_sum, up_sum)
     ortho = orthogonal_wide(gram, owned).reshape(2, 2, frows, D)
     ortho, pair_rows = lax.optimization_barrier((ortho, pair_rows))
     got = swap(ortho[1], x_bit, devices)
-    qkv_back, own = lax.optimization_barrier((qkv_back, ortho[0]))
+    qkv_back, out_far, own = lax.optimization_barrier((qkv_back, out_far, ortho[0]))
+    out_sum = out_near[0].astype(F32) + out_near[1].astype(F32) + out_far.astype(F32)
+    layer_out = jnp.where(live, hidden + out_sum, 0.0).astype(BF16)
     grad_bias = jnp.sum(qkv_back.astype(F32), axis=1)
     normed_one_grad = mm(qkv_back, w_qkv, ((0,), (1,)))
     input_norm_grad, grad_gain_first = norm_backward(inputs, scale_one, gain_first, normed_one_grad)

time: 554 us -> 561 us (1.013)
  waiting for transfers between devices: 128 us -> 142 us
    ppermute x62, waiting for transfers between devices: 126 us -> 140 us  [swap(): lax.ppermute(value, BOTH, [(index, index ^ mask) for index in range(devic...]
    unnamed x139 -> x137, local copies, waits for them, and re-layouts: 13.8 us -> 12.1 us
  transfers between devices with their start and end apart: 68 -> 68, of which waited for: 25 -> 23; matrix products, arithmetic and copies ran while one was open for 23% -> 22% of each run, Pallas kernels for 22% -> 21%
where the time goes in v1:
time: 561 us; the launch traced here: 556 us
  waiting for transfers between devices  142 us (25%)
  starting transfers between devices  130 us (23%)
  Pallas kernels  123 us (22%)
  other arithmetic  60.6 us (11%)
  local copies, waits for them, and re-layouts  41.1 us (7%)
  matrix products  40.9 us (7%)
  between operations  17.6 us (3%)
    ppermute x62, waiting for transfers between devices, swap(): lax.ppermute(value, BOTH, [(index, index ^ mask) for index in range(devic...  140 us
    ppermute x62, starting transfers between devices, swap(): lax.ppermute(value, BOTH, [(index, index ^ mask) for index in range(devic...  109 us
    pallas_call x2, Pallas kernels, feed_forward(): pl.pallas_call(body, grid=(2,), in_specs=in_specs, out_specs=[line(count)...  44.2 us
    dot_general x9, matrix products, mm(): lax.dot_general(left, right, (contract, ((), ())), preferred_element_type...  40.9 us
    pallas_call x1, Pallas kernels, orthogonal_whole(): pl.pallas_call(lambda *refs: whole_kernel(widths, *refs), out_shape=jax.S...  19.9 us
    pallas_call x4, Pallas kernels, attend_back(): pl.pallas_call(body, grid=(heads,), in_specs=[pl.BlockSpec(memory_space=p...  19.8 us
    pallas_call x1, Pallas kernels, orthogonal_wide(): pl.pallas_call(wide_kernel, out_shape=jax.ShapeDtypeStruct(rows.shape, BF...  17.9 us
    unnamed x137, local copies, waits for them, and re-layouts  12.1 us
  transfers between devices with their start and end apart: 68, of which 23 were waited for; matrix products, arithmetic and copies ran while one was open for 22% of the time, Pallas kernels for 21%

profile of v1, /device:TPU:0, one launch (start us, length us, event | category | flops | bytes accessed | tf_op | source)
XLA Modules:
  0.0 555.6 jit_solution(15137667961082234431)
XLA Ops:
  21.4 6.7 %collective-permute-done.4 = bf16[2,32,2048]{2,1,0:T(8,128)(2,1)S(1)} collective-permute-done((bf16[2,32,2048]{2,1,0:T(8,128)(2,1)S(1)}, bf16[2,32,2048]{2,1,0:T(8,128)(2,1)S(1)}, u32[]{:S(2)}, u32[]{:S(2)}) %collective-permute-start.4) | collective-permute-done | bytes 262176 | tf_op jit(solution)/shard_map/ppermute | solution.py:68
  30.0 10.5 %collective-permute-done.5 = bf16[2,2,32,2048]{3,2,0,1:T(8,128)(2,1)S(1)} collective-permute-done((bf16[2,2,32,2048]{3,2,0,1:T(8,128)(2,1)S(1)}, bf16[2,2,32,2048]{3,2,0,1:T(8,128)(2,1)S(1)}, u32[]{:S(2)}, u32[]{:S(2)}) %collective-permute-start.5) | collective-permute-done | bytes 524320 | tf_op jit(solution)/shard_map/ppermute | solution.py:68
  60.3 9.9 %collective-permute-done.12 = bf16[152,896]{1,0:T(8,128)(2,1)} collective-permute-done((bf16[152,896]{1,0:T(8,128)(2,1)S(1)}, bf16[152,896]{1,0:T(8,128)(2,1)}, u32[]{:S(2)}, u32[]{:S(2)}) %collective-permute-start.12) | collective-permute-done | bytes 272416 | tf_op jit(solution)/shard_map/ppermute | solution.py:68
  85.8 7.3 %collective-permute-done.9 = bf16[256,512]{1,0:T(8,128)(2,1)} collective-permute-done((bf16[256,512]{1,0:T(8,128)(2,1)}, bf16[256,512]{1,0:T(8,128)(2,1)}, u32[]{:S(2)}, u32[]{:S(2)}) %collective-permute-start.9) | collective-permute-done | bytes 262176 | tf_op jit(solution)/shard_map/ppermute | solution.py:68
  106.0 6.2 %collective-permute-done.14 = bf16[2,2,2,32,896]{4,3,0,2,1:T(8,128)(2,1)S(1)} collective-permute-done((bf16[2,2,2,32,896]{4,3,0,2,1:T(8,128)(2,1)S(1)}, bf16[2,2,2,32,896]{4,3,0,2,1:T(8,128)(2,1)S(1)}, u32[]{:S(2)}, u32[]{:S(2)}) %collective-permute-start.14) | collective-permute-done | bytes 458784 | tf_op jit(solution)/shard_map/ppermute | solution.py:68
  115.0 9.5 %collective-permute-start.15 = (bf16[512,896]{1,0:T(8,128)(2,1)}, bf16[512,896]{1,0:T(8,128)(2,1)S(1)}, u32[]{:S(2)}, u32[]{:S(2)}) collective-permute-start(bf16[512,896]{1,0:T(8,128)(2,1)} %bitcast_select_fusion.dy0), channel_id=1, source_target_pairs={{0,2},{1,3},{2,0},{3,1},{4,6},{5,7},{6,4},{7,5},{8,10},{9,11},{10,... | collective-permute-start | bytes 2752520 | tf_op jit(solution)/shard_map/ppermute | solution.py:68
  137.9 9.4 %collective-permute-done.16 = bf16[2,2,152,896]{3,2,1,0:T(8,128)(2,1)} collective-permute-done((bf16[2,2,152,896]{3,2,1,0:T(8,128)(2,1)}, bf16[2,2,152,896]{3,2,1,0:T(8,128)(2,1)}, u32[]{:S(2)}, u32[]{:S(2)}) %collective-permute-start.16) | collective-permute-done | bytes 1089568 | tf_op jit(solution)/shard_map/ppermute | solution.py:68
  164.3 22.0 %feed_forward.2 = (bf16[2048,1216]{1,0:T(8,128)(2,1)}, bf16[2048,2432]{1,0:T(8,128)(2,1)}, bf16[2048,896]{1,0:T(8,128)(2,1)}, bf16[2048,896]{1,0:T(8,128)(2,1)},...) custom-call(bf16[512,896]{1,0:T(8,128)(2,1)} %multiply_convert_fusion.x0, ...), custom_call_target="tpu_custom_call" | custom-call | flops 11156848640 | bytes 15712256 | tf_op jit(solution)/shard_map/feed_forward/pallas_call | solution.py:377
  188.3 7.1 %all-to-all-start = ((bf16[32,28,304]{2,1,0:T(8,128)(2,1)}), bf16[32,28,304]{2,1,0:T(8,128)(2,1)S(1)}, u32[]{:S(2)}, u32[]{:S(2)}) async-start(bf16[32,28,304]{2,1,0:T(8,128)(2,1)} %get-tuple-element.214), calls=%async_computation | async-start | bytes 1572864 | tf_op jit(solution)/shard_map/all_to_all | solution.py:881
  195.4 22.2 %feed_forward.3 = (bf16[2048,1216]{1,0:T(8,128)(2,1)}, bf16[2048,2432]{1,0:T(8,128)(2,1)}, bf16[2048,896]{1,0:T(8,128)(2,1)}, bf16[2048,896]{1,0:T(8,128)(2,1)},...) custom-call(bf16[512,896]{1,0:T(8,128)(2,1)} %collective-permute-don, ...), custom_call_target="tpu_custom_call", output_to_operand_aliasing={{0}: (6, {}), {1}: (7, {}), {2}: (8, {}), {3}: (9, {})} | custom-call | flops 11156848640 | bytes 15712256 | tf_op jit(solution)/shard_map/feed_forward/pallas_call | solution.py:377
  228.1 15.2 %convolution_convert_fusion = bf16[2432,896]{1,0:T(8,128)(2,1)S(1)} fusion(bf16[2048,2432]{1,0:T(8,128)(2,1)} %get-tuple-element.220, bf16[2048,896]{1,0:T(8,128)(2,1)} %get-tuple-element.221), kind=kOutput, calls=%fused_computation | convolution fusion | flops 8927657984 | bytes 17989632 | tf_op jit(solution)/shard_map/dot_general | solution.py:50
  299.6 6.2 %collective-permute-start.39 = (bf16[128,512]{1,0:T(8,128)(2,1)S(1)}, bf16[128,512]{1,0:T(8,128)(2,1)S(1)}, u32[]{:S(2)}, u32[]{:S(2)}) collective-permute-start(bf16[128,512]{1,0:T(8,128)(2,1)S(1)} %dynamic-slice_bitcast_fusion.43), channel_id=1, source_target_pairs={{0,2},{1,3},{2,0},{3,1},{4,6},{5,7},{6,4},{7,5},{8,10},{9,11},{10,... | collective-permute-start | bytes 393224 | tf_op jit(solution)/shard_map/ppermute | solution.py:68
  335.1 13.9 %collective-permute-start.41 = (bf16[128,512]{1,0:T(8,128)(2,1)S(1)}, bf16[128,512]{1,0:T(8,128)(2,1)S(1)}, u32[]{:S(2)}, u32[]{:S(2)}) collective-permute-start(bf16[128,512]{1,0:T(8,128)(2,1)S(1)} %dynamic-slice_bitcast_fusion.42), channel_id=1, source_target_pairs={{0,2},{1,3},{2,0},{3,1},{4,6},{5,7},{6,4},{7,5},{8,10},{9,11},{10,... | collective-permute-start | bytes 393224 | tf_op jit(solution)/shard_map/ppermute | solution.py:68
  361.9 6.7 %collective-permute-start.49 = (bf16[2,152,896]{2,1,0:T(8,128)(2,1)S(1)}, bf16[2,152,896]{2,1,0:T(8,128)(2,1)S(1)}, u32[]{:S(2)}, u32[]{:S(2)}) collective-permute-start(bf16[2,152,896]{2,1,0:T(8,128)(2,1)S(1)} %get-tuple-element.357), channel_id=1, source_target_pairs={{0,2},{1,3},{2,0},{3,1},{4,6},{5,7},{6,4},{7,5},{8,10},{9,11},{10,... | collective-permute-start | bytes 1634312 | tf_op jit(solution)/shard_map/ppermute | solution.py:68
  368.6 12.4 %collective-permute-done.49 = bf16[2,152,896]{2,1,0:T(8,128)(2,1)S(1)} collective-permute-done((bf16[2,152,896]{2,1,0:T(8,128)(2,1)S(1)}, bf16[2,152,896]{2,1,0:T(8,128)(2,1)S(1)}, u32[]{:S(2)}, u32[]{:S(2)}) %collective-permute-start.49) | collective-permute-done | bytes 544800 | tf_op jit(solution)/shard_map/ppermute | solution.py:68
  385.4 6.2 %collective-permute-done.50 = bf16[2,2,32,1152]{3,2,1,0:T(8,128)(2,1)S(1)} collective-permute-done((bf16[2,2,32,1152]{3,2,1,0:T(8,128)(2,1)S(1)}, bf16[2,2,32,1152]{3,2,1,0:T(8,128)(2,1)S(1)}, u32[]{:S(2)}, u32[]{:S(2)}) %collective-permute-start.50) | collective-permute-done | bytes 294944 | tf_op jit(solution)/shard_map/ppermute | solution.py:68
  397.9 7.5 %collective-permute-done.52 = bf16[2,32,1152]{2,1,0:T(8,128)(2,1)S(1)} collective-permute-done((bf16[2,32,1152]{2,1,0:T(8,128)(2,1)S(1)}, bf16[2,32,1152]{2,1,0:T(8,128)(2,1)S(1)}, u32[]{:S(2)}, u32[]{:S(2)}) %collective-permute-start.52) | collective-permute-done | bytes 147488 | tf_op jit(solution)/shard_map/ppermute | solution.py:68
  408.7 6.7 %collective-permute-done.54 = bf16[32,1152]{1,0:T(8,128)(2,1)S(1)} collective-permute-done((bf16[32,1152]{1,0:T(8,128)(2,1)S(1)}, bf16[32,1152]{1,0:T(8,128)(2,1)S(1)}, u32[]{:S(2)}, u32[]{:S(2)}) %collective-permute-start.54) | collective-permute-done | bytes 73760 | tf_op jit(solution)/shard_map/ppermute | solution.py:68
  416.2 7.8 %collective-permute-done.57 = bf16[4,128,128]{2,1,0:T(8,128)(2,1)S(1)} collective-permute-done((bf16[4,128,128]{2,1,0:T(8,128)(2,1)S(1)}, bf16[4,128,128]{2,1,0:T(8,128)(2,1)S(1)}, u32[]{:S(2)}, u32[]{:S(2)}) %collective-permute-start.57) | collective-permute-done | bytes 131104 | tf_op jit(solution)/shard_map/ppermute | solution.py:68
  424.3 7.6 %collective-permute-done.58 = bf16[2,4,128,128]{3,2,1,0:T(8,128)(2,1)S(1)} collective-permute-done((bf16[2,4,128,128]{3,2,1,0:T(8,128)(2,1)S(1)}, bf16[2,4,128,128]{3,2,1,0:T(8,128)(2,1)S(1)}, u32[]{:S(2)}, u32[]{:S(2)}) %collective-permute-start.58) | collective-permute-done | bytes 262176 | tf_op jit(solution)/shard_map/ppermute | solution.py:68
  436.6 9.1 %collective-permute-done.59 = bf16[2,2,4,128,128]{4,3,2,0,1:T(8,128)(2,1)} collective-permute-done((bf16[2,2,4,128,128]{4,3,2,0,1:T(8,128)(2,1)}, bf16[2,2,4,128,128]{4,3,2,0,1:T(8,128)(2,1)}, u32[]{:S(2)}, u32[]{:S(2)}) %collective-permute-start.59) | collective-permute-done | bytes 524320 | tf_op jit(solution)/shard_map/ppermute | solution.py:68
  456.5 17.9 %newton_wide.1 = bf16[608,896]{1,0:T(8,128)(2,1)S(1)} custom-call(bf16[32,128,128]{2,1,0:T(8,128)(2,1)S(1)} %bitcast.363, bf16[608,896]{1,0:T(8,128)(2,1)S(1)} %bitcast.359), custom_call_target="tpu_custom_call" | custom-call | flops 10070523904 | bytes 2179072 | tf_op jit(solution)/shard_map/newton_wide/pallas_call | solution.py:482
  478.8 11.3 %collective-permute-done.56 = bf16[512,896]{1,0:T(8,128)(2,1)} collective-permute-done((bf16[512,896]{1,0:T(8,128)(2,1)}, bf16[512,896]{1,0:T(8,128)(2,1)}, u32[]{:S(2)}, u32[]{:S(2)}) %collective-permute-start.56) | collective-permute-done | bytes 917536 | tf_op jit(solution)/shard_map/ppermute | solution.py:68
  521.4 19.9 %newton_whole.1.refs_1_ = bf16[32,1152]{1,0:T(8,128)(2,1)S(1)} custom-call(bf16[1024,1152]{1,0:T(8,128)(2,1)S(1)} %copy-done.10, f32[32,1152]{1,0:T(8,128)S(1)} %get-tuple-element.328.refs_1_), custom_call_target="tpu_custom_call" | custom-call | flops 11576279040 | bytes 2359296 | tf_op jit(solution)/shard_map/newton_whole/pallas_call | solution.py:515
  (461 shorter events, 278.7 us)
Async XLA Ops:
  7.2 157.2 %all-gather.3.cloned.1.call-start = ((), (), s32[]{:S(2)}) async-start(), calls=%async_computation.4 | async-start | bytes 4902912 | tf_op jit(solution)/shard_map/all_gather | solution.py:777
  15.0 32.6 %collective-permute-start.2 = (bf16[28,2432]{1,0:T(8,128)(2,1)}, bf16[28,2432]{1,0:T(8,128)(2,1)}, u32[]{:S(2)}, u32[]{:S(2)}) collective-permute-start(bf16[28,2432]{1,0:T(8,128)(2,1)} %get-tuple-element.396), channel_id=1, source_target_pairs={{0,3},{1,2},{2,1},{3,0},{4,7},{5,6},{6,5},{7,4},{8,11},{9,10},{10,... | collective-permute-start | bytes 408584 | tf_op jit(solution)/shard_map/ppermute | solution.py:68
  15.7 35.4 %collective-permute-start.1 = (bf16[28,2432]{1,0:T(8,128)(2,1)}, bf16[28,2432]{1,0:T(8,128)(2,1)}, u32[]{:S(2)}, u32[]{:S(2)}) collective-permute-start(bf16[28,2432]{1,0:T(8,128)(2,1)} %get-tuple-element.397), channel_id=1, source_target_pairs={{0,2},{1,3},{2,0},{3,1},{4,6},{5,7},{6,4},{7,5},{8,10},{9,11},{10,... | collective-permute-start | bytes 408584 | tf_op jit(solution)/shard_map/ppermute | solution.py:68
  16.5 34.6 %collective-permute-start = (bf16[28,2432]{1,0:T(8,128)(2,1)}, bf16[28,2432]{1,0:T(8,128)(2,1)}, u32[]{:S(2)}, u32[]{:S(2)}) collective-permute-start(bf16[28,2432]{1,0:T(8,128)(2,1)} %get-tuple-element.398), channel_id=1, source_target_pairs={{0,1},{1,0},{2,3},{3,2},{4,5},{5,4},{6,7},{7,6},{8,9},{9,8},{10,11... | collective-permute-start | bytes 408584 | tf_op jit(solution)/shard_map/ppermute | solution.py:68
  113.3 34.1 %collective-permute-start.16 = (bf16[2,2,152,896]{3,2,1,0:T(8,128)(2,1)}, bf16[2,2,152,896]{3,2,1,0:T(8,128)(2,1)}, u32[]{:S(2)}, u32[]{:S(2)}) collective-permute-start(bf16[2,2,152,896]{3,2,1,0:T(8,128)(2,1)} %bitcast.37), channel_id=1, source_target_pairs={{0,4},{1,5},{2,6},{3,7},{4,0},{5,1},{6,2},{7,3},{8,12},{9,13},{10,... | collective-permute-start | bytes 3268616 | tf_op jit(solution)/shard_map/ppermute | solution.py:68
  115.0 32.4 %collective-permute-start.15 = (bf16[512,896]{1,0:T(8,128)(2,1)}, bf16[512,896]{1,0:T(8,128)(2,1)S(1)}, u32[]{:S(2)}, u32[]{:S(2)}) collective-permute-start(bf16[512,896]{1,0:T(8,128)(2,1)} %bitcast_select_fusion.dy0), channel_id=1, source_target_pairs={{0,2},{1,3},{2,0},{3,1},{4,6},{5,7},{6,4},{7,5},{8,10},{9,11},{10,... | collective-permute-start | bytes 2752520 | tf_op jit(solution)/shard_map/ppermute | solution.py:68
  130.0 33.1 %collective-permute-start.20 = (bf16[512,896]{1,0:T(8,128)(2,1)}, bf16[512,896]{1,0:T(8,128)(2,1)}, u32[]{:S(2)}, u32[]{:S(2)}) collective-permute-start(bf16[512,896]{1,0:T(8,128)(2,1)} %bitcast_select_fusion.dy0), channel_id=1, source_target_pairs={{0,1},{1,0},{2,3},{3,2},{4,5},{5,4},{6,7},{7,6},{8,9},{9,8},{10,11... | collective-permute-start | bytes 2752520 | tf_op jit(solution)/shard_map/ppermute | solution.py:68
  188.3 29.3 %all-to-all-start = ((bf16[32,28,304]{2,1,0:T(8,128)(2,1)}), bf16[32,28,304]{2,1,0:T(8,128)(2,1)S(1)}, u32[]{:S(2)}, u32[]{:S(2)}) async-start(bf16[32,28,304]{2,1,0:T(8,128)(2,1)} %get-tuple-element.214), calls=%async_computation | async-start | bytes 1572864 | tf_op jit(solution)/shard_map/all_to_all | solution.py:881
  195.3 324.4 %all-gather.5.cloned.1.call-start = ((), (), s32[]{:S(2)}) async-start(), calls=%async_computation.5 | async-start | bytes 2433024 | tf_op jit(solution)/shard_map/all_gather | solution.py:1012
  224.3 30.1 %collective-permute-start.25 = (bf16[512,896]{1,0:T(8,128)(2,1)}, bf16[512,896]{1,0:T(8,128)(2,1)S(1)}, u32[]{:S(2)}, u32[]{:S(2)}) collective-permute-start(bf16[512,896]{1,0:T(8,128)(2,1)} %get-tuple-element.223), channel_id=1, source_target_pairs={{0,1},{1,0},{2,3},{3,2},{4,5},{5,4},{6,7},{7,6},{8,9},{9,8},{10,11... | collective-permute-start | bytes 2752520 | tf_op jit(solution)/shard_map/ppermute | solution.py:68
  226.3 28.2 %collective-permute-start.26 = (bf16[512,896]{1,0:T(8,128)(2,1)S(1)}, bf16[512,896]{1,0:T(8,128)(2,1)S(1)}, u32[]{:S(2)}, u32[]{:S(2)}) collective-permute-start(bf16[512,896]{1,0:T(8,128)(2,1)S(1)} %add_convert_fusion.6), channel_id=1, source_target_pairs={{0,2},{1,3},{2,0},{3,1},{4,6},{5,7},{6,4},{7,5},{8,10},{9,11},{10,... | collective-permute-start | bytes 2752520 | tf_op jit(solution)/shard_map/ppermute | solution.py:68
  243.9 27.3 %collective-permute-start.27 = (bf16[2,2,152,896]{3,2,1,0:T(8,128)(2,1)S(1)}, bf16[2,2,152,896]{3,2,1,0:T(8,128)(2,1)S(1)}, u32[]{:S(2)}, u32[]{:S(2)}) collective-permute-start(bf16[2,2,152,896]{3,2,1,0:T(8,128)(2,1)S(1)} %get-tuple-element.338), channel_id=1, source_target_pairs={{0,4},{1,5},{2,6},{3,7},{4,0},{5,1},{6,2},{7,3},{8,12},{9,13},{10,... | collective-permute-start | bytes 3268616 | tf_op jit(solution)/shard_map/ppermute | solution.py:68
  245.7 25.6 %collective-permute-start.24 = (bf16[2,2,152,896]{3,2,1,0:T(8,128)(2,1)S(1)}, bf16[2,2,152,896]{3,2,1,0:T(8,128)(2,1)S(1)}, u32[]{:S(2)}, u32[]{:S(2)}) collective-permute-start(bf16[2,2,152,896]{3,2,1,0:T(8,128)(2,1)S(1)} %get-tuple-element.340), channel_id=1, source_target_pairs={{0,8},{1,9},{2,10},{3,11},{4,12},{5,13},{6,14},{7,15},{8,0},{9,1},... | collective-permute-start | bytes 3268616 | tf_op jit(solution)/shard_map/ppermute | solution.py:68
  253.4 44.6 %collective-permute-start.31 = (bf16[2,2,152,896]{3,2,1,0:T(8,128)(2,1)S(1)}, bf16[2,2,152,896]{3,2,1,0:T(8,128)(2,1)S(1)}, u32[]{:S(2)}, u32[]{:S(2)}) collective-permute-start(bf16[2,2,152,896]{3,2,1,0:T(8,128)(2,1)S(1)} %get-tuple-element.336), channel_id=1, source_target_pairs={{0,4},{1,5},{2,6},{3,7},{4,0},{5,1},{6,2},{7,3},{8,12},{9,13},{10,... | collective-permute-start | bytes 3268616 | tf_op jit(solution)/shard_map/ppermute | solution.py:68
  271.7 46.5 %collective-permute-start.33 = (bf16[2,152,896]{2,1,0:T(8,128)(2,1)S(1)}, bf16[2,152,896]{2,1,0:T(8,128)(2,1)S(1)}, u32[]{:S(2)}, u32[]{:S(2)}) collective-permute-start(bf16[2,152,896]{2,1,0:T(8,128)(2,1)S(1)} %get-tuple-element.364), channel_id=1, source_target_pairs={{0,8},{1,9},{2,10},{3,11},{4,12},{5,13},{6,14},{7,15},{8,0},{9,1},... | collective-permute-start | bytes 1634312 | tf_op jit(solution)/shard_map/ppermute | solution.py:68
  273.6 44.6 %collective-permute-start.34 = (bf16[2,152,896]{2,1,0:T(8,128)(2,1)S(1)}, bf16[2,152,896]{2,1,0:T(8,128)(2,1)S(1)}, u32[]{:S(2)}, u32[]{:S(2)}) collective-permute-start(bf16[2,152,896]{2,1,0:T(8,128)(2,1)S(1)} %get-tuple-element.365), channel_id=1, source_target_pairs={{0,16},{1,17},{2,18},{3,19},{4,20},{5,21},{6,22},{7,23},{8,24},{9,... | collective-permute-start | bytes 1634312 | tf_op jit(solution)/shard_map/ppermute | solution.py:68
  276.5 34.0 %collective-permute-start.30 = (bf16[2,2,2,32,896]{4,3,2,1,0:T(8,128)(2,1)S(1)}, bf16[2,2,2,32,896]{4,3,2,1,0:T(8,128)(2,1)S(1)}, u32[]{:S(2)}, u32[]{:S(2)}) collective-permute-start(bf16[2,2,2,32,896]{4,3,2,1,0:T(8,128)(2,1)S(1)} %get-tuple-element.385), channel_id=1, source_target_pairs={{0,2},{1,3},{2,0},{3,1},{4,6},{5,7},{6,4},{7,5},{8,10},{9,11},{10,... | collective-permute-start | bytes 1376264 | tf_op jit(solution)/shard_map/ppermute | solution.py:68
  320.1 36.4 %collective-permute-start.42 = (bf16[152,896]{1,0:T(8,128)(2,1)S(1)}, bf16[152,896]{1,0:T(8,128)(2,1)S(1)}, u32[]{:S(2)}, u32[]{:S(2)}) collective-permute-start(bf16[152,896]{1,0:T(8,128)(2,1)S(1)} %get-tuple-element.407), channel_id=1, source_target_pairs={{0,16},{1,17},{2,18},{3,19},{4,20},{5,21},{6,22},{7,23},{8,24},{9,... | collective-permute-start | bytes 817160 | tf_op jit(solution)/shard_map/ppermute | solution.py:68
  320.8 35.7 %collective-permute-start.43 = (bf16[152,896]{1,0:T(8,128)(2,1)S(1)}, bf16[152,896]{1,0:T(8,128)(2,1)S(1)}, u32[]{:S(2)}, u32[]{:S(2)}) collective-permute-start(bf16[152,896]{1,0:T(8,128)(2,1)S(1)} %get-tuple-element.405), channel_id=1, source_target_pairs={{0,4},{1,5},{2,6},{3,7},{4,0},{5,1},{6,2},{7,3},{8,12},{9,13},{10,... | collective-permute-start | bytes 817160 | tf_op jit(solution)/shard_map/ppermute | solution.py:68
  424.2 76.9 %collective-permute-start.29 = (bf16[512,896]{1,0:T(8,128)(2,1)}, bf16[512,896]{1,0:T(8,128)(2,1)}, u32[]{:S(2)}, u32[]{:S(2)}) collective-permute-start(bf16[512,896]{1,0:T(8,128)(2,1)} %get-tuple-element.332), channel_id=1, source_target_pairs={{0,1},{1,0},{2,3},{3,2},{4,5},{5,4},{6,7},{7,6},{8,9},{9,8},{10,11... | collective-permute-start | bytes 2752520 | tf_op jit(solution)/shard_map/ppermute | solution.py:68
  449.1 27.2 %all-to-all-start.1 = ((bf16[32,28,304]{2,1,0:T(8,128)(2,1)}), bf16[32,28,304]{2,1,0:T(8,128)(2,1)S(1)}, u32[]{:S(2)}, u32[]{:S(2)}) async-start(bf16[32,28,304]{2,1,0:T(8,128)(2,1)} %turn.2), calls=%async_computation.1 | async-start | bytes 1572864 | tf_op jit(solution)/shard_map/all_to_all | solution.py:780
  454.8 35.4 %collective-permute-start.56 = (bf16[512,896]{1,0:T(8,128)(2,1)}, bf16[512,896]{1,0:T(8,128)(2,1)}, u32[]{:S(2)}, u32[]{:S(2)}) collective-permute-start(bf16[512,896]{1,0:T(8,128)(2,1)} %add_convert_fusion.4), channel_id=1, source_target_pairs={{0,2},{1,3},{2,0},{3,1},{4,6},{5,7},{6,4},{7,5},{8,10},{9,11},{10,... | collective-permute-start | bytes 2752520 | tf_op jit(solution)/shard_map/ppermute | solution.py:68
  477.4 27.4 %collective-permute-start.60 = (bf16[2,152,896]{2,1,0:T(8,128)(2,1)}, bf16[2,152,896]{2,1,0:T(8,128)(2,1)S(1)}, u32[]{:S(2)}, u32[]{:S(2)}) collective-permute-start(bf16[2,152,896]{2,1,0:T(8,128)(2,1)} %get-tuple-element.355), channel_id=1, source_target_pairs={{0,2},{1,3},{2,0},{3,1},{4,6},{5,7},{6,4},{7,5},{8,10},{9,11},{10,... | collective-permute-start | bytes 1634312 | tf_op jit(solution)/shard_map/ppermute | solution.py:68
  513.6 27.8 %all-to-all-start.3 = ((bf16[32,28,304]{2,1,0:T(8,128)(2,1)}), bf16[32,28,304]{2,1,0:T(8,128)(2,1)S(1)}, u32[]{:S(2)}, u32[]{:S(2)}) async-start(bf16[32,28,304]{2,1,0:T(8,128)(2,1)} %turn.3), calls=%async_computation.3 | async-start | bytes 1572864 | tf_op jit(solution)/shard_map/all_to_all | solution.py:1050
  (109 other events, 1149.7 us)
Sparse Core Ops, SparseCore 0:
  60.4 83.4 all-gather.2
  435.6 62.2 all-gather.4
